TPU v7x, 128 devices: a whole 4x4x4 slice. The times are simulated.
128 devices in a mesh: outer: 16 (over x, z), inner: 8 (over y, core).
Axes of the slice: x: 4, y: 4, z: 4, core: 2. Of those that a mesh axis runs over, the one named last changes fastest.
Arguments:
- shocks: bfloat16 [16, 1048576], P(None, ('outer', 'inner')), may hold values from -6 to 6
- leaf_basis: bfloat16 [4096, 32, 256], P(('outer', 'inner')), may hold values from -0.375 to 0.375
- self_block: bfloat16 [4096, 256, 256], P(('outer', 'inner')), may hold values from -0.25 to 0.25
- near_block: bfloat16 [4096, 3, 256, 256], P(('outer', 'inner')), may hold values from -0.25 to 0.25
- near_offset: int32 [4096, 3], P(('outer', 'inner')), may hold values from -32 to 32
- near_count: int32 [4096], P(('outer', 'inner')), may hold values from 0 to 3
- local_transfer: bfloat16 [8064, 1024], P(('outer', 'inner')), may hold values from -0.75 to 0.75
- local_coupling: bfloat16 [8064, 8, 1024], P(('outer', 'inner')), may hold values from -1 to 1
- far_device: int32 [8064, 8], P(('outer', 'inner')), may hold values from 0 to 127, as said below
- far_slot: int32 [8064, 8], P(('outer', 'inner')), may hold values from 0 to 62, as said below
- upper_transfer: bfloat16 [120, 1024], replicated, may hold values from -0.75 to 0.75
- upper_coupling: bfloat16 [124, 8, 1024], replicated, may hold values from -1 to 1
- upper_partner: int32 [124, 8], replicated, may hold values from 4 to 127, as said below
Outputs:
- hazard_field: float32 [16, 1048576], P(None, ('outer', 'inner'))
Inputs may be any that keep to these rules, and one draw needn't show every extreme that they name: `far_device`: for a row of a level-k cluster held by device d, every entry is within min(2^(k+1), 32) of d; on some device each level's rows reach that distance. `far_slot`: each entry is the row, among the 63 clusters held by the target device (levels in order, leaves first), of a cluster on the same level as the row's own cluster. `upper_partner`: row h - 4 lists nodes of the same level as upper node h (nodes 2^j .. 2^(j+1) - 1), never h itself.
All inputs are finite; a program needn't handle non-finite values.
Results may differ from a plain program's by a relative error of at most 0.0027.
Values may be sent and summed in bfloat16 or wider, within the bound.
A program may use at most 128 MiB of HBM per device.

v0:
```python
import jax
import jax.numpy as jnp
from jax import lax
from jax.sharding import PartitionSpec as P

PRECISE = lax.Precision.HIGHEST


def padded(array, sides, width):
    for axis, dim in sides:
        size, length = (lax.axis_size(axis), array.shape[dim])
        up = [(i, (i + 1) % size) for i in range(size - 1)]
        down = [(j, i) for i, j in up]
        last = lax.slice_in_dim(array, length - width, length, axis=dim)
        first = lax.slice_in_dim(array, 0, width, axis=dim)
        before = lax.ppermute(last, axis, up)
        after = lax.ppermute(first, axis, down)
        array = jnp.concatenate([before, array, after], axis=dim)
    return array


def from_behind(array, axis, by):
    size = lax.axis_size(axis)
    pairs = [(i, i + by) for i in range(size) if 0 <= i + by < size]
    return lax.ppermute(array, axis, pairs)


def level_rows(height, leaf_count):
    extent = leaf_count >> height
    return (2 * leaf_count - 2 * extent, extent)


def pair_sum(products):
    return products.reshape(products.shape[0] // 2, 2, products.shape[1], products.shape[2]).sum(
        axis=1
    )


def apply_rows(coefficients, matrices):
    return jnp.einsum("nsr,nrq->nsq", coefficients, matrices, precision=PRECISE)


def apply_back(coefficients, matrices):
    return jnp.einsum("nsq,nrq->nsr", coefficients, matrices, precision=PRECISE)


def slab_start(distance, far_reach, leaves):
    level_up = 0
    while min(2 << level_up, far_reach) < distance:
        level_up = level_up + 1
    return level_rows(level_up, leaves)[0]


def local(
    shocks,
    leaf_basis,
    self_block,
    near_block,
    near_offset,
    near_count,
    local_transfer,
    local_coupling,
    far_device,
    far_slot,
    upper_transfer,
    upper_coupling,
    upper_partner,
):
    scenarios, width_dev = shocks.shape
    leaves, rank_dim, leaf_len = leaf_basis.shape
    near_slots = near_block.shape[1]
    cluster_rows, partners, matrix_len = local_coupling.shape
    devices = lax.axis_size(("outer", "inner"))
    heights = leaves.bit_length() - 1
    top_height = devices.bit_length() - 1
    blocks = shocks.reshape(scenarios, leaves, leaf_len)
    self_sum = jnp.einsum("snp,npq->snq", blocks, self_block, preferred_element_type=jnp.float32)
    extended = padded(shocks, ((("outer", "inner"), 1),), width_dev)
    widened = extended.reshape(scenarios, 3 * leaves, leaf_len)
    near_index = jnp.arange(leaves, dtype=jnp.int32)[:, None] + near_offset + leaves
    live_mask = jnp.arange(near_slots, dtype=jnp.int32)[None, :] < near_count[:, None]
    picked = jnp.take(widened, near_index.reshape(-1), axis=1).reshape(
        scenarios, leaves, near_slots, leaf_len
    )
    picked = jnp.where(live_mask[None, :, :, None], picked, jnp.zeros((), jnp.bfloat16))
    near_sum = self_sum + jnp.einsum(
        "snkp,nkpq->snq", picked, near_block, preferred_element_type=jnp.float32
    )
    leaf_coef = jnp.einsum("snp,nrp->nsr", blocks, leaf_basis, preferred_element_type=jnp.float32)
    transfer = local_transfer.astype(jnp.float32).reshape(cluster_rows, rank_dim, rank_dim)
    tiers = [leaf_coef]
    for height in range(1, heights + 1):
        offset, extent = level_rows(height - 1, leaves)
        tiers.append(pair_sum(apply_rows(tiers[-1], transfer[offset : offset + extent])))
    root_matrix = transfer[cluster_rows - 1 :]
    lifted = apply_rows(tiers[-1], root_matrix)
    upper_matrix = upper_transfer.astype(jnp.float32).reshape(-1, rank_dim, rank_dim)
    root_terms = lax.all_gather(lifted, ("outer", "inner"), axis=0, tiled=True)
    current = pair_sum(root_terms)
    by_height = {top_height - 1: current}
    low_height = top_height - 1
    for height in range(low_height, 2, -1):
        first = 2**height - 8
        current = pair_sum(apply_rows(current, upper_matrix[first : first + 2**height]))
        by_height[height - 1] = current
    every_node = jnp.concatenate(
        [jnp.zeros((4, scenarios, rank_dim), jnp.float32)]
        + [by_height[height] for height in range(2, top_height)],
        axis=0,
    )
    couple_up = upper_coupling.astype(jnp.float32).reshape(
        upper_coupling.shape[0], partners, rank_dim, rank_dim
    )
    upper_field = jnp.einsum(
        "nfsr,nfrq->nsq", every_node[upper_partner], couple_up, precision=PRECISE
    )
    upper_down = upper_field[0:4]
    for height in range(3, top_height):
        first = 2**height
        parent = jnp.repeat(upper_down, 2, axis=0)
        upper_down = upper_field[first - 4 : 2 * first - 4] + apply_back(
            parent, upper_matrix[first - 8 : 2 * first - 8]
        )
    device_index = lax.axis_index(("outer", "inner"))
    parent_field = lax.dynamic_slice_in_dim(upper_down, device_index // 2, 1, 0)
    root_down = apply_back(parent_field, root_matrix)
    cluster_coef = jnp.concatenate(tiers, axis=0)
    couple_local = local_coupling.astype(jnp.float32).reshape(
        cluster_rows, partners, rank_dim, rank_dim
    )
    products = jnp.einsum("nsr,nfrq->nfsq", cluster_coef, couple_local, precision=PRECISE)
    products = products.reshape(cluster_rows * partners, scenarios * rank_dim)
    far_reach = min(2 * leaves, devices // 4)
    starts = {}
    layout = {}
    row_shift = {0: 0}
    position = cluster_rows
    for heading in (1, -1):
        for distance in range(1, far_reach + 1):
            begin = slab_start(distance, far_reach, leaves)
            starts[distance] = begin
            layout[heading, distance] = position
            row_shift[heading * distance] = position - begin
            position = position + cluster_rows - begin
    shift_table = jnp.array(
        [row_shift[value] for value in range(-far_reach, far_reach + 1)], jnp.int32
    )
    relative = far_device.reshape(-1) - device_index
    matches = (
        relative[:, None] == jnp.arange(-far_reach, far_reach + 1, dtype=jnp.int32)[None, :]
    ).astype(jnp.int32)
    row_target = far_slot.reshape(-1) + jnp.sum(matches * shift_table[None, :], axis=1)
    chooser = (row_target[None, :] == jnp.arange(position, dtype=jnp.int32)[:, None]).astype(
        jnp.float32
    )
    assembled = jnp.dot(chooser, products, precision=PRECISE)
    local_field = assembled[:cluster_rows]
    for heading in (1, -1):
        for distance in range(1, far_reach + 1):
            begin = layout[heading, distance]
            slab = assembled[begin : begin + cluster_rows - starts[distance]]
            arrived = from_behind(slab, ("outer", "inner"), heading * distance)
            local_field = local_field.at[starts[distance] :].add(arrived)
    local_field = local_field.reshape(cluster_rows, scenarios, rank_dim)
    cluster_field = local_field[cluster_rows - 1 :] + root_down
    for height in range(heights - 1, -1, -1):
        offset, extent = level_rows(height, leaves)
        parent = jnp.repeat(cluster_field, 2, axis=0)
        cluster_field = local_field[offset : offset + extent] + apply_back(
            parent, transfer[offset : offset + extent]
        )
    leaf_field = cluster_field.astype(jnp.bfloat16)
    far_part = jnp.einsum(
        "nsr,nrp->snp", leaf_field, leaf_basis, preferred_element_type=jnp.float32
    )
    return (near_sum + far_part).reshape(scenarios, width_dev)


def solution(mesh):
    placed = (
        P(None, ("outer", "inner")),
        P(("outer", "inner"), None, None),
        P(("outer", "inner"), None, None),
        P(("outer", "inner"), None, None, None),
        P(("outer", "inner"), None),
        P(("outer", "inner")),
        P(("outer", "inner"), None),
        P(("outer", "inner"), None, None),
        P(("outer", "inner"), None),
        P(("outer", "inner"), None),
        P(),
        P(),
        P(),
    )
    return jax.shard_map(
        local, mesh=mesh, in_specs=placed, out_specs=P(None, ("outer", "inner")), check_vma=False
    )
```

profile of v0, /device:TPU:1, one launch (start us, length us, event | category | flops | bytes accessed | tf_op | source)
XLA Modules:
  0.0 577.4 jit_solution(5801259234816614761)
XLA Ops:
  10.3 7.6 %copy.123 = bf16[63,8,32,32]{3,2,1,0:T(8,128)(2,1)} copy(bf16[63,8,32,32]{0,3,2,1:T(8,128)(2,1)S(1)} %bitcast.130) | data formatting | bytes 2064384 | tf_op jit(solution)/shard_map/reshape | solution.py:128
  37.1 10.9 %collective-permute-start.3 = (f32[63,512]{1,0:T(8,128)}, f32[63,512]{1,0:T(8,128)}, u32[]{:S(2)}, u32[]{:S(2)}) collective-permute-start(f32[63,512]{1,0:T(8,128)} %get-tuple-element.884), channel_id=1, source_target_pairs={{0,2},{1,3},{2,4},{3,5},{4,6},{5,7},{6,8},{7,9},{8,10},{9,11},{10,... | collective-permute-start | bytes 387080 | tf_op jit(solution)/shard_map/ppermute | solution.py:25
  48.7 10.1 %collective-permute-start.4 = (f32[31,512]{1,0:T(8,128)}, f32[31,512]{1,0:T(8,128)}, u32[]{:S(2)}, u32[]{:S(2)}) collective-permute-start(f32[31,512]{1,0:T(8,128)} %get-tuple-element.881), channel_id=1, source_target_pairs={{0,3},{1,4},{2,5},{3,6},{4,7},{5,8},{6,9},{7,10},{8,11},{9,12},{10... | collective-permute-start | bytes 190472 | tf_op jit(solution)/shard_map/ppermute | solution.py:25
  58.8 10.2 %collective-permute-start.5 = (f32[31,512]{1,0:T(8,128)}, f32[31,512]{1,0:T(8,128)}, u32[]{:S(2)}, u32[]{:S(2)}) collective-permute-start(f32[31,512]{1,0:T(8,128)} %get-tuple-element.880), channel_id=1, source_target_pairs={{0,4},{1,5},{2,6},{3,7},{4,8},{5,9},{6,10},{7,11},{8,12},{9,13},{1... | collective-permute-start | bytes 190472 | tf_op jit(solution)/shard_map/ppermute | solution.py:25
  69.8 10.2 %collective-permute-start.6 = (f32[15,512]{1,0:T(8,128)}, f32[15,512]{1,0:T(8,128)}, u32[]{:S(2)}, u32[]{:S(2)}) collective-permute-start(f32[15,512]{1,0:T(8,128)} %get-tuple-element.877), channel_id=1, source_target_pairs={{0,5},{1,6},{2,7},{3,8},{4,9},{5,10},{6,11},{7,12},{8,13},{9,14},{... | collective-permute-start | bytes 92168 | tf_op jit(solution)/shard_map/ppermute | solution.py:25
  87.3 40.4 %all-gather = f32[2048,32]{1,0:T(8,128)} all-gather(f32[16,32]{1,0:T(8,128)S(1)} %fusion.49), channel_id=2, replica_groups=mesh['outer'=16,'inner'=8] {'outer','inner'}, dimensions={0}, use_global_device_ids=true | all-gather | bytes 264192 | tf_op jit(solution)/shard_map/all_gather | solution.py:98
  153.8 13.1 %copy.128 = bf16[124,8,32,32]{3,2,1,0:T(8,128)(2,1)} copy(bf16[124,8,32,32]{0,3,2,1:T(8,128)(2,1)} %bitcast.131) | data formatting | bytes 4063232 | tf_op jit(solution)/shard_map/reshape | solution.py:111
  168.1 10.4 %gather_fusion.1 = f32[992,16,32]{2,1,0:T(8,128)} fusion(f32[128,16,32]{2,1,0:T(8,128)S(1)} %constant_dynamic-update-slice_fusion.6, s32[1024]{0:T(1024)S(1)} %get-tuple-element.903), kind=kCustom, calls=%fused_computation.1 | custom fusion | bytes 4067200 | tf_op jit(solution)/shard_map/gather | solution.py:115
  178.6 13.2 %convolution_bitcast_fusion.1 = f32[124,16,32]{2,1,0:T(8,128)S(1)} fusion(f32[124,8,16,32]{3,2,1,0:T(8,128)} %bitcast.129, bf16[124,8,32,32]{3,2,1,0:T(8,128)(2,1)} %copy.128), kind=kOutput, calls=%fused_computation.5 | convolution fusion | flops 195035136 | bytes 4317184 | tf_op jit(solution)/shard_map/nfsr,nfrq->nsq/dot_general | solution.py:114
  210.0 10.2 %collective-permute-start.8 = (f32[15,512]{1,0:T(8,128)}, f32[15,512]{1,0:T(8,128)S(1)}, u32[]{:S(2)}, u32[]{:S(2)}) collective-permute-start(f32[15,512]{1,0:T(8,128)} %get-tuple-element.875), channel_id=1, source_target_pairs={{0,7},{1,8},{2,9},{3,10},{4,11},{5,12},{6,13},{7,14},{8,15},{9,16}... | collective-permute-start | bytes 92168 | tf_op jit(solution)/shard_map/ppermute | solution.py:25
  221.3 10.2 %collective-permute-start.9 = (f32[15,512]{1,0:T(8,128)S(1)}, f32[15,512]{1,0:T(8,128)S(1)}, u32[]{:S(2)}, u32[]{:S(2)}) collective-permute-start(f32[15,512]{1,0:T(8,128)S(1)} %copy-done.13), channel_id=1, source_target_pairs={{0,8},{1,9},{2,10},{3,11},{4,12},{5,13},{6,14},{7,15},{8,16},{9,17... | collective-permute-start | bytes 92168 | tf_op jit(solution)/shard_map/ppermute | solution.py:25
  232.3 10.2 %collective-permute-start.10 = (f32[7,512]{1,0:T(8,128)}, f32[7,512]{1,0:T(8,128)S(1)}, u32[]{:S(2)}, u32[]{:S(2)}) collective-permute-start(f32[7,512]{1,0:T(8,128)} %get-tuple-element.869), channel_id=1, source_target_pairs={{0,9},{1,10},{2,11},{3,12},{4,13},{5,14},{6,15},{7,16},{8,17},{9,1... | collective-permute-start | bytes 43016 | tf_op jit(solution)/shard_map/ppermute | solution.py:25
  243.4 10.2 %collective-permute-start.11 = (f32[7,512]{1,0:T(8,128)S(1)}, f32[7,512]{1,0:T(8,128)S(1)}, u32[]{:S(2)}, u32[]{:S(2)}) collective-permute-start(f32[7,512]{1,0:T(8,128)S(1)} %copy-done.22), channel_id=1, source_target_pairs={{0,10},{1,11},{2,12},{3,13},{4,14},{5,15},{6,16},{7,17},{8,18},{9,... | collective-permute-start | bytes 43016 | tf_op jit(solution)/shard_map/ppermute | solution.py:25
  254.4 10.2 %collective-permute-start.12 = (f32[7,512]{1,0:T(8,128)S(1)}, f32[7,512]{1,0:T(8,128)S(1)}, u32[]{:S(2)}, u32[]{:S(2)}) collective-permute-start(f32[7,512]{1,0:T(8,128)S(1)} %copy-done.21), channel_id=1, source_target_pairs={{0,11},{1,12},{2,13},{3,14},{4,15},{5,16},{6,17},{7,18},{8,19},{9,... | collective-permute-start | bytes 43016 | tf_op jit(solution)/shard_map/ppermute | solution.py:25
  265.4 10.2 %collective-permute-start.13 = (f32[7,512]{1,0:T(8,128)S(1)}, f32[7,512]{1,0:T(8,128)S(1)}, u32[]{:S(2)}, u32[]{:S(2)}) collective-permute-start(f32[7,512]{1,0:T(8,128)S(1)} %copy-done.20), channel_id=1, source_target_pairs={{0,12},{1,13},{2,14},{3,15},{4,16},{5,17},{6,18},{7,19},{8,20},{9,... | collective-permute-start | bytes 43016 | tf_op jit(solution)/shard_map/ppermute | solution.py:25
  275.6 10.2 %collective-permute-start.14 = (f32[7,512]{1,0:T(8,128)S(1)}, f32[7,512]{1,0:T(8,128)S(1)}, u32[]{:S(2)}, u32[]{:S(2)}) collective-permute-start(f32[7,512]{1,0:T(8,128)S(1)} %copy-done.19), channel_id=1, source_target_pairs={{0,13},{1,14},{2,15},{3,16},{4,17},{5,18},{6,19},{7,20},{8,21},{9,... | collective-permute-start | bytes 43016 | tf_op jit(solution)/shard_map/ppermute | solution.py:25
  285.8 10.2 %collective-permute-start.15 = (f32[7,512]{1,0:T(8,128)S(1)}, f32[7,512]{1,0:T(8,128)S(1)}, u32[]{:S(2)}, u32[]{:S(2)}) collective-permute-start(f32[7,512]{1,0:T(8,128)S(1)} %copy-done.18), channel_id=1, source_target_pairs={{0,14},{1,15},{2,16},{3,17},{4,18},{5,19},{6,20},{7,21},{8,22},{9,... | collective-permute-start | bytes 43016 | tf_op jit(solution)/shard_map/ppermute | solution.py:25
  296.0 10.2 %collective-permute-start.16 = (f32[7,512]{1,0:T(8,128)S(1)}, f32[7,512]{1,0:T(8,128)S(1)}, u32[]{:S(2)}, u32[]{:S(2)}) collective-permute-start(f32[7,512]{1,0:T(8,128)S(1)} %copy-done.17), channel_id=1, source_target_pairs={{0,15},{1,16},{2,17},{3,18},{4,19},{5,20},{6,21},{7,22},{8,23},{9,... | collective-permute-start | bytes 43016 | tf_op jit(solution)/shard_map/ppermute | solution.py:25
  375.2 17.1 %collective-permute-start.36 = (f32[31,512]{1,0:T(8,128)}, f32[31,512]{1,0:T(8,128)S(1)}, u32[]{:S(2)}, u32[]{:S(2)}) collective-permute-start(f32[31,512]{1,0:T(8,128)} %get-tuple-element.879), channel_id=1, source_target_pairs={{3,0},{4,1},{5,2},{6,3},{7,4},{8,5},{9,6},{10,7},{11,8},{12,9},{13... | collective-permute-start | bytes 190472 | tf_op jit(solution)/shard_map/ppermute | solution.py:25
  401.8 14.2 %collective-permute-start.37 = (f32[31,512]{1,0:T(8,128)S(1)}, f32[31,512]{1,0:T(8,128)S(1)}, u32[]{:S(2)}, u32[]{:S(2)}) collective-permute-start(f32[31,512]{1,0:T(8,128)S(1)} %copy-done.12), channel_id=1, source_target_pairs={{4,0},{5,1},{6,2},{7,3},{8,4},{9,5},{10,6},{11,7},{12,8},{13,9},{1... | collective-permute-start | bytes 190472 | tf_op jit(solution)/shard_map/ppermute | solution.py:25
  416.0 10.2 %collective-permute-start.42 = (f32[7,512]{1,0:T(8,128)}, f32[7,512]{1,0:T(8,128)S(1)}, u32[]{:S(2)}, u32[]{:S(2)}) collective-permute-start(f32[7,512]{1,0:T(8,128)} %get-tuple-element.854), channel_id=1, source_target_pairs={{9,0},{10,1},{11,2},{12,3},{13,4},{14,5},{15,6},{16,7},{17,8},{18,... | collective-permute-start | bytes 43016 | tf_op jit(solution)/shard_map/ppermute | solution.py:25
  426.2 10.2 %collective-permute-start.43 = (f32[7,512]{1,0:T(8,128)}, f32[7,512]{1,0:T(8,128)S(1)}, u32[]{:S(2)}, u32[]{:S(2)}) collective-permute-start(f32[7,512]{1,0:T(8,128)} %get-tuple-element.861), channel_id=1, source_target_pairs={{10,0},{11,1},{12,2},{13,3},{14,4},{15,5},{16,6},{17,7},{18,8},{19... | collective-permute-start | bytes 43016 | tf_op jit(solution)/shard_map/ppermute | solution.py:25
  444.4 9.8 %collective-permute-start.38 = (f32[15,512]{1,0:T(8,128)}, f32[15,512]{1,0:T(8,128)S(1)}, u32[]{:S(2)}, u32[]{:S(2)}) collective-permute-start(f32[15,512]{1,0:T(8,128)} %get-tuple-element.870), channel_id=1, source_target_pairs={{5,0},{6,1},{7,2},{8,3},{9,4},{10,5},{11,6},{12,7},{13,8},{14,9},{... | collective-permute-start | bytes 92168 | tf_op jit(solution)/shard_map/ppermute | solution.py:25
  454.2 10.2 %collective-permute-start.39 = (f32[15,512]{1,0:T(8,128)}, f32[15,512]{1,0:T(8,128)S(1)}, u32[]{:S(2)}, u32[]{:S(2)}) collective-permute-start(f32[15,512]{1,0:T(8,128)} %get-tuple-element.873), channel_id=1, source_target_pairs={{6,0},{7,1},{8,2},{9,3},{10,4},{11,5},{12,6},{13,7},{14,8},{15,9},... | collective-permute-start | bytes 92168 | tf_op jit(solution)/shard_map/ppermute | solution.py:25
  464.4 10.2 %collective-permute-start.40 = (f32[15,512]{1,0:T(8,128)}, f32[15,512]{1,0:T(8,128)S(1)}, u32[]{:S(2)}, u32[]{:S(2)}) collective-permute-start(f32[15,512]{1,0:T(8,128)} %get-tuple-element.872), channel_id=1, source_target_pairs={{7,0},{8,1},{9,2},{10,3},{11,4},{12,5},{13,6},{14,7},{15,8},{16,9}... | collective-permute-start | bytes 92168 | tf_op jit(solution)/shard_map/ppermute | solution.py:25
  474.6 10.2 %collective-permute-start.41 = (f32[15,512]{1,0:T(8,128)}, f32[15,512]{1,0:T(8,128)S(1)}, u32[]{:S(2)}, u32[]{:S(2)}) collective-permute-start(f32[15,512]{1,0:T(8,128)} %get-tuple-element.871), channel_id=1, source_target_pairs={{8,0},{9,1},{10,2},{11,3},{12,4},{13,5},{14,6},{15,7},{16,8},{17,9... | collective-permute-start | bytes 92168 | tf_op jit(solution)/shard_map/ppermute | solution.py:25
  484.8 10.2 %collective-permute-start.44 = (f32[7,512]{1,0:T(8,128)}, f32[7,512]{1,0:T(8,128)S(1)}, u32[]{:S(2)}, u32[]{:S(2)}) collective-permute-start(f32[7,512]{1,0:T(8,128)} %get-tuple-element.860), channel_id=1, source_target_pairs={{11,0},{12,1},{13,2},{14,3},{15,4},{16,5},{17,6},{18,7},{19,8},{20... | collective-permute-start | bytes 43016 | tf_op jit(solution)/shard_map/ppermute | solution.py:25
  501.5 7.1 %collective-permute-start.45 = (f32[7,512]{1,0:T(8,128)}, f32[7,512]{1,0:T(8,128)S(1)}, u32[]{:S(2)}, u32[]{:S(2)}) collective-permute-start(f32[7,512]{1,0:T(8,128)} %get-tuple-element.859), channel_id=1, source_target_pairs={{12,0},{13,1},{14,2},{15,3},{16,4},{17,5},{18,6},{19,7},{20,8},{21... | collective-permute-start | bytes 43016 | tf_op jit(solution)/shard_map/ppermute | solution.py:25
  508.6 10.2 %collective-permute-start.46 = (f32[7,512]{1,0:T(8,128)}, f32[7,512]{1,0:T(8,128)S(1)}, u32[]{:S(2)}, u32[]{:S(2)}) collective-permute-start(f32[7,512]{1,0:T(8,128)} %get-tuple-element.858), channel_id=1, source_target_pairs={{13,0},{14,1},{15,2},{16,3},{17,4},{18,5},{19,6},{20,7},{21,8},{22... | collective-permute-start | bytes 43016 | tf_op jit(solution)/shard_map/ppermute | solution.py:25
  518.8 10.2 %collective-permute-start.47 = (f32[7,512]{1,0:T(8,128)}, f32[7,512]{1,0:T(8,128)S(1)}, u32[]{:S(2)}, u32[]{:S(2)}) collective-permute-start(f32[7,512]{1,0:T(8,128)} %get-tuple-element.857), channel_id=1, source_target_pairs={{14,0},{15,1},{16,2},{17,3},{18,4},{19,5},{20,6},{21,7},{22,8},{23... | collective-permute-start | bytes 43016 | tf_op jit(solution)/shard_map/ppermute | solution.py:25
  529.0 10.2 %collective-permute-start.48 = (f32[7,512]{1,0:T(8,128)}, f32[7,512]{1,0:T(8,128)S(1)}, u32[]{:S(2)}, u32[]{:S(2)}) collective-permute-start(f32[7,512]{1,0:T(8,128)} %get-tuple-element.856), channel_id=1, source_target_pairs={{15,0},{16,1},{17,2},{18,3},{19,4},{20,5},{21,6},{22,7},{23,8},{24... | collective-permute-start | bytes 43016 | tf_op jit(solution)/shard_map/ppermute | solution.py:25
  539.2 10.2 %collective-permute-start.49 = (f32[7,512]{1,0:T(8,128)S(1)}, f32[7,512]{1,0:T(8,128)S(1)}, u32[]{:S(2)}, u32[]{:S(2)}) collective-permute-start(f32[7,512]{1,0:T(8,128)S(1)} %copy-done.15), channel_id=1, source_target_pairs={{16,0},{17,1},{18,2},{19,3},{20,4},{21,5},{22,6},{23,7},{24,8},{25... | collective-permute-start | bytes 43016 | tf_op jit(solution)/shard_map/ppermute | solution.py:25
  (317 shorter events, 207.9 us)
Async XLA Ops:
  32.5 171.3 %collective-permute-start.2 = (f32[63,512]{1,0:T(8,128)}, f32[63,512]{1,0:T(8,128)}, u32[]{:S(2)}, u32[]{:S(2)}) collective-permute-start(f32[63,512]{1,0:T(8,128)} %get-tuple-element.885), channel_id=1, source_target_pairs={{0,1},{1,2},{2,3},{3,4},{4,5},{5,6},{6,7},{7,8},{8,9},{9,10},{10,1... | collective-permute-start | bytes 387080 | tf_op jit(solution)/shard_map/ppermute | solution.py:25
  37.1 172.9 %collective-permute-start.3 = (f32[63,512]{1,0:T(8,128)}, f32[63,512]{1,0:T(8,128)}, u32[]{:S(2)}, u32[]{:S(2)}) collective-permute-start(f32[63,512]{1,0:T(8,128)} %get-tuple-element.884), channel_id=1, source_target_pairs={{0,2},{1,3},{2,4},{3,5},{4,6},{5,7},{6,8},{7,9},{8,10},{9,11},{10,... | collective-permute-start | bytes 387080 | tf_op jit(solution)/shard_map/ppermute | solution.py:25
  48.7 172.5 %collective-permute-start.4 = (f32[31,512]{1,0:T(8,128)}, f32[31,512]{1,0:T(8,128)}, u32[]{:S(2)}, u32[]{:S(2)}) collective-permute-start(f32[31,512]{1,0:T(8,128)} %get-tuple-element.881), channel_id=1, source_target_pairs={{0,3},{1,4},{2,5},{3,6},{4,7},{5,8},{6,9},{7,10},{8,11},{9,12},{10... | collective-permute-start | bytes 190472 | tf_op jit(solution)/shard_map/ppermute | solution.py:25
  58.8 173.5 %collective-permute-start.5 = (f32[31,512]{1,0:T(8,128)}, f32[31,512]{1,0:T(8,128)}, u32[]{:S(2)}, u32[]{:S(2)}) collective-permute-start(f32[31,512]{1,0:T(8,128)} %get-tuple-element.880), channel_id=1, source_target_pairs={{0,4},{1,5},{2,6},{3,7},{4,8},{5,9},{6,10},{7,11},{8,12},{9,13},{1... | collective-permute-start | bytes 190472 | tf_op jit(solution)/shard_map/ppermute | solution.py:25
  69.8 173.6 %collective-permute-start.6 = (f32[15,512]{1,0:T(8,128)}, f32[15,512]{1,0:T(8,128)}, u32[]{:S(2)}, u32[]{:S(2)}) collective-permute-start(f32[15,512]{1,0:T(8,128)} %get-tuple-element.877), channel_id=1, source_target_pairs={{0,5},{1,6},{2,7},{3,8},{4,9},{5,10},{6,11},{7,12},{8,13},{9,14},{... | collective-permute-start | bytes 92168 | tf_op jit(solution)/shard_map/ppermute | solution.py:25
  203.8 50.6 %collective-permute-start.7 = (f32[15,512]{1,0:T(8,128)}, f32[15,512]{1,0:T(8,128)S(1)}, u32[]{:S(2)}, u32[]{:S(2)}) collective-permute-start(f32[15,512]{1,0:T(8,128)} %get-tuple-element.876), channel_id=1, source_target_pairs={{0,6},{1,7},{2,8},{3,9},{4,10},{5,11},{6,12},{7,13},{8,14},{9,15},... | collective-permute-start | bytes 92168 | tf_op jit(solution)/shard_map/ppermute | solution.py:25
  210.0 55.3 %collective-permute-start.8 = (f32[15,512]{1,0:T(8,128)}, f32[15,512]{1,0:T(8,128)S(1)}, u32[]{:S(2)}, u32[]{:S(2)}) collective-permute-start(f32[15,512]{1,0:T(8,128)} %get-tuple-element.875), channel_id=1, source_target_pairs={{0,7},{1,8},{2,9},{3,10},{4,11},{5,12},{6,13},{7,14},{8,15},{9,16}... | collective-permute-start | bytes 92168 | tf_op jit(solution)/shard_map/ppermute | solution.py:25
  221.3 54.3 %collective-permute-start.9 = (f32[15,512]{1,0:T(8,128)S(1)}, f32[15,512]{1,0:T(8,128)S(1)}, u32[]{:S(2)}, u32[]{:S(2)}) collective-permute-start(f32[15,512]{1,0:T(8,128)S(1)} %copy-done.13), channel_id=1, source_target_pairs={{0,8},{1,9},{2,10},{3,11},{4,12},{5,13},{6,14},{7,15},{8,16},{9,17... | collective-permute-start | bytes 92168 | tf_op jit(solution)/shard_map/ppermute | solution.py:25
  232.3 53.5 %collective-permute-start.10 = (f32[7,512]{1,0:T(8,128)}, f32[7,512]{1,0:T(8,128)S(1)}, u32[]{:S(2)}, u32[]{:S(2)}) collective-permute-start(f32[7,512]{1,0:T(8,128)} %get-tuple-element.869), channel_id=1, source_target_pairs={{0,9},{1,10},{2,11},{3,12},{4,13},{5,14},{6,15},{7,16},{8,17},{9,1... | collective-permute-start | bytes 43016 | tf_op jit(solution)/shard_map/ppermute | solution.py:25
  243.4 52.6 %collective-permute-start.11 = (f32[7,512]{1,0:T(8,128)S(1)}, f32[7,512]{1,0:T(8,128)S(1)}, u32[]{:S(2)}, u32[]{:S(2)}) collective-permute-start(f32[7,512]{1,0:T(8,128)S(1)} %copy-done.22), channel_id=1, source_target_pairs={{0,10},{1,11},{2,12},{3,13},{4,14},{5,15},{6,16},{7,17},{8,18},{9,... | collective-permute-start | bytes 43016 | tf_op jit(solution)/shard_map/ppermute | solution.py:25
  254.4 51.8 %collective-permute-start.12 = (f32[7,512]{1,0:T(8,128)S(1)}, f32[7,512]{1,0:T(8,128)S(1)}, u32[]{:S(2)}, u32[]{:S(2)}) collective-permute-start(f32[7,512]{1,0:T(8,128)S(1)} %copy-done.21), channel_id=1, source_target_pairs={{0,11},{1,12},{2,13},{3,14},{4,15},{5,16},{6,17},{7,18},{8,19},{9,... | collective-permute-start | bytes 43016 | tf_op jit(solution)/shard_map/ppermute | solution.py:25
  265.4 46.1 %collective-permute-start.13 = (f32[7,512]{1,0:T(8,128)S(1)}, f32[7,512]{1,0:T(8,128)S(1)}, u32[]{:S(2)}, u32[]{:S(2)}) collective-permute-start(f32[7,512]{1,0:T(8,128)S(1)} %copy-done.20), channel_id=1, source_target_pairs={{0,12},{1,13},{2,14},{3,15},{4,16},{5,17},{6,18},{7,19},{8,20},{9,... | collective-permute-start | bytes 43016 | tf_op jit(solution)/shard_map/ppermute | solution.py:25
  275.6 40.0 %collective-permute-start.14 = (f32[7,512]{1,0:T(8,128)S(1)}, f32[7,512]{1,0:T(8,128)S(1)}, u32[]{:S(2)}, u32[]{:S(2)}) collective-permute-start(f32[7,512]{1,0:T(8,128)S(1)} %copy-done.19), channel_id=1, source_target_pairs={{0,13},{1,14},{2,15},{3,16},{4,17},{5,18},{6,19},{7,20},{8,21},{9,... | collective-permute-start | bytes 43016 | tf_op jit(solution)/shard_map/ppermute | solution.py:25
  285.8 35.9 %collective-permute-start.15 = (f32[7,512]{1,0:T(8,128)S(1)}, f32[7,512]{1,0:T(8,128)S(1)}, u32[]{:S(2)}, u32[]{:S(2)}) collective-permute-start(f32[7,512]{1,0:T(8,128)S(1)} %copy-done.18), channel_id=1, source_target_pairs={{0,14},{1,15},{2,16},{3,17},{4,18},{5,19},{6,20},{7,21},{8,22},{9,... | collective-permute-start | bytes 43016 | tf_op jit(solution)/shard_map/ppermute | solution.py:25
  296.0 29.6 %collective-permute-start.16 = (f32[7,512]{1,0:T(8,128)S(1)}, f32[7,512]{1,0:T(8,128)S(1)}, u32[]{:S(2)}, u32[]{:S(2)}) collective-permute-start(f32[7,512]{1,0:T(8,128)S(1)} %copy-done.17), channel_id=1, source_target_pairs={{0,15},{1,16},{2,17},{3,18},{4,19},{5,20},{6,21},{7,22},{8,23},{9,... | collective-permute-start | bytes 43016 | tf_op jit(solution)/shard_map/ppermute | solution.py:25
  306.2 24.0 %collective-permute-start.17 = (f32[7,512]{1,0:T(8,128)S(1)}, f32[7,512]{1,0:T(8,128)S(1)}, u32[]{:S(2)}, u32[]{:S(2)}) collective-permute-start(f32[7,512]{1,0:T(8,128)S(1)} %copy-done.16), channel_id=1, source_target_pairs={{0,16},{1,17},{2,18},{3,19},{4,20},{5,21},{6,22},{7,23},{8,24},{9,... | collective-permute-start | bytes 43016 | tf_op jit(solution)/shard_map/ppermute | solution.py:25
  356.3 38.6 %collective-permute-start.34 = (f32[63,512]{1,0:T(8,128)}, f32[63,512]{1,0:T(8,128)S(1)}, u32[]{:S(2)}, u32[]{:S(2)}) collective-permute-start(f32[63,512]{1,0:T(8,128)} %get-tuple-element.882), channel_id=1, source_target_pairs={{1,0},{2,1},{3,2},{4,3},{5,4},{6,5},{7,6},{8,7},{9,8},{10,9},{11,1... | collective-permute-start | bytes 387080 | tf_op jit(solution)/shard_map/ppermute | solution.py:25
  359.3 37.0 %collective-permute-start.35 = (f32[63,512]{1,0:T(8,128)}, f32[63,512]{1,0:T(8,128)S(1)}, u32[]{:S(2)}, u32[]{:S(2)}) collective-permute-start(f32[63,512]{1,0:T(8,128)} %get-tuple-element.883), channel_id=1, source_target_pairs={{2,0},{3,1},{4,2},{5,3},{6,4},{7,5},{8,6},{9,7},{10,8},{11,9},{12,... | collective-permute-start | bytes 387080 | tf_op jit(solution)/shard_map/ppermute | solution.py:25
  375.2 62.4 %collective-permute-start.36 = (f32[31,512]{1,0:T(8,128)}, f32[31,512]{1,0:T(8,128)S(1)}, u32[]{:S(2)}, u32[]{:S(2)}) collective-permute-start(f32[31,512]{1,0:T(8,128)} %get-tuple-element.879), channel_id=1, source_target_pairs={{3,0},{4,1},{5,2},{6,3},{7,4},{8,5},{9,6},{10,7},{11,8},{12,9},{13... | collective-permute-start | bytes 190472 | tf_op jit(solution)/shard_map/ppermute | solution.py:25
  395.0 31.2 %collective-permute-start.57 = (f32[3,512]{1,0:T(4,128)}, f32[3,512]{1,0:T(4,128)S(1)}, u32[]{:S(2)}, u32[]{:S(2)}) collective-permute-start(f32[3,512]{1,0:T(4,128)} %get-tuple-element.844), channel_id=1, source_target_pairs={{24,0},{25,1},{26,2},{27,3},{28,4},{29,5},{30,6},{31,7},{32,8},{33... | collective-permute-start | bytes 18440 | tf_op jit(solution)/shard_map/ppermute | solution.py:25
  396.3 40.1 %collective-permute-start.58 = (f32[3,512]{1,0:T(4,128)}, f32[3,512]{1,0:T(4,128)S(1)}, u32[]{:S(2)}, u32[]{:S(2)}) collective-permute-start(f32[3,512]{1,0:T(4,128)} %get-tuple-element.843), channel_id=1, source_target_pairs={{25,0},{26,1},{27,2},{28,3},{29,4},{30,5},{31,6},{32,7},{33,8},{34... | collective-permute-start | bytes 18440 | tf_op jit(solution)/shard_map/ppermute | solution.py:25
  401.8 83.0 %collective-permute-start.37 = (f32[31,512]{1,0:T(8,128)S(1)}, f32[31,512]{1,0:T(8,128)S(1)}, u32[]{:S(2)}, u32[]{:S(2)}) collective-permute-start(f32[31,512]{1,0:T(8,128)S(1)} %copy-done.12), channel_id=1, source_target_pairs={{4,0},{5,1},{6,2},{7,3},{8,4},{9,5},{10,6},{11,7},{12,8},{13,9},{1... | collective-permute-start | bytes 190472 | tf_op jit(solution)/shard_map/ppermute | solution.py:25
  416.0 48.4 %collective-permute-start.42 = (f32[7,512]{1,0:T(8,128)}, f32[7,512]{1,0:T(8,128)S(1)}, u32[]{:S(2)}, u32[]{:S(2)}) collective-permute-start(f32[7,512]{1,0:T(8,128)} %get-tuple-element.854), channel_id=1, source_target_pairs={{9,0},{10,1},{11,2},{12,3},{13,4},{14,5},{15,6},{16,7},{17,8},{18,... | collective-permute-start | bytes 43016 | tf_op jit(solution)/shard_map/ppermute | solution.py:25
  426.2 48.4 %collective-permute-start.43 = (f32[7,512]{1,0:T(8,128)}, f32[7,512]{1,0:T(8,128)S(1)}, u32[]{:S(2)}, u32[]{:S(2)}) collective-permute-start(f32[7,512]{1,0:T(8,128)} %get-tuple-element.861), channel_id=1, source_target_pairs={{10,0},{11,1},{12,2},{13,3},{14,4},{15,5},{16,6},{17,7},{18,8},{19... | collective-permute-start | bytes 43016 | tf_op jit(solution)/shard_map/ppermute | solution.py:25
  444.4 64.2 %collective-permute-start.38 = (f32[15,512]{1,0:T(8,128)}, f32[15,512]{1,0:T(8,128)S(1)}, u32[]{:S(2)}, u32[]{:S(2)}) collective-permute-start(f32[15,512]{1,0:T(8,128)} %get-tuple-element.870), channel_id=1, source_target_pairs={{5,0},{6,1},{7,2},{8,3},{9,4},{10,5},{11,6},{12,7},{13,8},{14,9},{... | collective-permute-start | bytes 92168 | tf_op jit(solution)/shard_map/ppermute | solution.py:25
  454.2 64.6 %collective-permute-start.39 = (f32[15,512]{1,0:T(8,128)}, f32[15,512]{1,0:T(8,128)S(1)}, u32[]{:S(2)}, u32[]{:S(2)}) collective-permute-start(f32[15,512]{1,0:T(8,128)} %get-tuple-element.873), channel_id=1, source_target_pairs={{6,0},{7,1},{8,2},{9,3},{10,4},{11,5},{12,6},{13,7},{14,8},{15,9},... | collective-permute-start | bytes 92168 | tf_op jit(solution)/shard_map/ppermute | solution.py:25
  464.4 64.6 %collective-permute-start.40 = (f32[15,512]{1,0:T(8,128)}, f32[15,512]{1,0:T(8,128)S(1)}, u32[]{:S(2)}, u32[]{:S(2)}) collective-permute-start(f32[15,512]{1,0:T(8,128)} %get-tuple-element.872), channel_id=1, source_target_pairs={{7,0},{8,1},{9,2},{10,3},{11,4},{12,5},{13,6},{14,7},{15,8},{16,9}... | collective-permute-start | bytes 92168 | tf_op jit(solution)/shard_map/ppermute | solution.py:25
  474.6 64.6 %collective-permute-start.41 = (f32[15,512]{1,0:T(8,128)}, f32[15,512]{1,0:T(8,128)S(1)}, u32[]{:S(2)}, u32[]{:S(2)}) collective-permute-start(f32[15,512]{1,0:T(8,128)} %get-tuple-element.871), channel_id=1, source_target_pairs={{8,0},{9,1},{10,2},{11,3},{12,4},{13,5},{14,6},{15,7},{16,8},{17,9... | collective-permute-start | bytes 92168 | tf_op jit(solution)/shard_map/ppermute | solution.py:25
  501.5 47.9 %collective-permute-start.45 = (f32[7,512]{1,0:T(8,128)}, f32[7,512]{1,0:T(8,128)S(1)}, u32[]{:S(2)}, u32[]{:S(2)}) collective-permute-start(f32[7,512]{1,0:T(8,128)} %get-tuple-element.859), channel_id=1, source_target_pairs={{12,0},{13,1},{14,2},{15,3},{16,4},{17,5},{18,6},{19,7},{20,8},{21... | collective-permute-start | bytes 43016 | tf_op jit(solution)/shard_map/ppermute | solution.py:25
  508.6 42.1 %collective-permute-start.46 = (f32[7,512]{1,0:T(8,128)}, f32[7,512]{1,0:T(8,128)S(1)}, u32[]{:S(2)}, u32[]{:S(2)}) collective-permute-start(f32[7,512]{1,0:T(8,128)} %get-tuple-element.858), channel_id=1, source_target_pairs={{13,0},{14,1},{15,2},{16,3},{17,4},{18,5},{19,6},{20,7},{21,8},{22... | collective-permute-start | bytes 43016 | tf_op jit(solution)/shard_map/ppermute | solution.py:25
  518.8 33.2 %collective-permute-start.47 = (f32[7,512]{1,0:T(8,128)}, f32[7,512]{1,0:T(8,128)S(1)}, u32[]{:S(2)}, u32[]{:S(2)}) collective-permute-start(f32[7,512]{1,0:T(8,128)} %get-tuple-element.857), channel_id=1, source_target_pairs={{14,0},{15,1},{16,2},{17,3},{18,4},{19,5},{20,6},{21,7},{22,8},{23... | collective-permute-start | bytes 43016 | tf_op jit(solution)/shard_map/ppermute | solution.py:25
  529.0 24.4 %collective-permute-start.48 = (f32[7,512]{1,0:T(8,128)}, f32[7,512]{1,0:T(8,128)S(1)}, u32[]{:S(2)}, u32[]{:S(2)}) collective-permute-start(f32[7,512]{1,0:T(8,128)} %get-tuple-element.856), channel_id=1, source_target_pairs={{15,0},{16,1},{17,2},{18,3},{19,4},{20,5},{21,6},{22,7},{23,8},{24... | collective-permute-start | bytes 43016 | tf_op jit(solution)/shard_map/ppermute | solution.py:25
  (62 other events, 3137.0 us)
where the time goes:
time: 587 us; the launch traced here: 577 us
  starting transfers between devices  374 us (64%)
  local copies, waits for them, and re-layouts  75 us (13%)
  matrix products  45.9 us (8%)
  blocking collectives  40.4 us (7%)
  waiting for transfers between devices  30.1 us (5%)
  other arithmetic  10.3 us (2%)
    ppermute x64, starting transfers between devices, from_behind(): return lax.ppermute(array, axis, pairs)  369 us
    all_gather x1, blocking collectives, local(): root_terms = lax.all_gather(lifted, ('outer', 'inner'), axis=0, tiled=True)  40.4 us
    ppermute x64, waiting for transfers between devices, from_behind(): return lax.ppermute(array, axis, pairs)  27.1 us
    dot_general x1, matrix products, local(): jnp.einsum('nfsr,nfrq->nsq', every_node[upper_partner], couple_up, precis...  13.2 us
    reshape x1, local copies, waits for them, and re-layouts, local(): upper_coupling.astype(jnp.float32)  13.1 us
    slice x8, local copies, waits for them, and re-layouts, local(): upper_matrix[first:first + 2 ** height]  13 us
  transfers between devices with their start and end apart: 66, of which 8 were waited for; matrix products, arithmetic and copies ran while one was open for 16% of the time, Pallas kernels for 0%

commit v1 on v0

v1 whole, which is shorter than its diff:
```python
import jax
import jax.numpy as jnp
import numpy as np
from jax import lax
from jax.experimental import pallas as pl
from jax.experimental.pallas import tpu as pltpu
from jax.sharding import PartitionSpec as P

F32 = jnp.float32
BF16 = jnp.bfloat16
MESH = pl.DeviceIdType.MESH
VMEM = pl.BlockSpec(memory_space=pltpu.VMEM)
SMEM = pl.BlockSpec(memory_space=pltpu.SMEM)
ANY = pl.BlockSpec(memory_space=pl.ANY)

CLASSES = ((1, 2, 16, 0), (3, 4, 8, 64), (5, 8, 4, 96), (9, 16, 2, 128), (17, 32, 1, 160))
TILES = 192
MESSAGES = 64


def slot_of(offset):
    for near, far, tiles, base in CLASSES:
        if near <= abs(offset) <= far:
            count = far - near + 1
            place = offset + far if offset < 0 else offset - near + count
            return base + place * tiles
    return None


LEVEL_ROW = (0, 32, 48, 56, 60, 62, 63)


def lane_table():
    table = np.zeros((8, 768), np.int32)
    for lane in range(768):
        if lane < 256:
            item, part, scale, shift = lane, 0, 32, 64
        elif lane < 384:
            item, part, scale, shift = lane, 0, 16, 64 - 32
        elif lane < 512:
            item, part = 384 + (lane - 384) % 64, (lane - 384) // 64
            scale, shift = 16, 128 + 8 * part - 48
        elif lane < 640:
            item, part = 448 + (lane - 512) % 32, (lane - 512) // 32
            scale, shift = 16, 256 + 4 * part - 56
        else:
            item, part = 480 + (lane - 640) % 32, (lane - 640) // 32
            scale, shift = 16, 512 + 4 * part - 60
        if item >= 504:
            scale, shift = 0, -1000000
        table[0, lane], table[1, lane], table[2, lane], table[3, lane] = item // 8, item % 8, scale, shift
    return table


LANES = lane_table()
SPREAD = (np.arange(256)[:, None] % 32 == np.arange(1024)[None, :] // 32).astype(np.float32)
GATHER = (np.arange(1024)[:, None] // 32 == np.arange(128)[None, :] % 32).astype(np.float32)
SELECT = (np.arange(256)[:, None] % 32 == np.arange(128)[None, :] % 32).astype(np.float32)


def iota(shape, dim):
    return lax.broadcasted_iota(jnp.int32, shape, dim)


def halves(x):
    high = x.astype(BF16)
    low = (x - high.astype(F32)).astype(BF16)
    return high, low


def dot(a, b):
    return jnp.dot(a, b, preferred_element_type=F32)


def spread(coefs, mask, matrix):
    high, low = halves(jnp.where(mask, coefs, 0.0))
    return dot(jnp.concatenate([high, low], axis=1), matrix)


def fold(x):
    x = x + pltpu.roll(x, 64, 1)
    return x + pltpu.roll(x, 32, 1)


def apply(wide, row):
    total = wide[:, 0:128] * row[:, 0:128]
    for t in range(1, 8):
        total = total + wide[:, t * 128 : t * 128 + 128] * row[:, t * 128 : t * 128 + 128]
    return total


def first_group(rows):
    return iota((rows, 128), 1) < 32


def up_kernel(
    x_ref, v_ref, e_ref, b_ref, fd_ref, fs_ref, ut_ref, rr_ref, lane_ref,
    send_ref, own_ref, lift_ref, f_ref,
    ef_ref, uf_ref, wide_ref, prod_ref,
):
    outer = lax.axis_index("outer")
    me = outer * 8 + lax.axis_index("inner")
    matrix = rr_ref[...]
    ef_ref[pl.ds(0, 63), :] = e_ref[...].astype(F32)
    uf_ref[...] = ut_ref[...].astype(F32)
    for k in range(4):
        f_ref[k : k + 1, :] = uf_ref[pl.ds(56 + 4 * outer + k, 1), :]
    for k in range(2):
        f_ref[4 + k : 5 + k, :] = uf_ref[pl.ds(24 + 2 * outer + k, 1), :]

    group_mask = iota((64, 128), 1) // 32 == iota((64, 128), 0) // 16
    for group in range(8):
        block = jnp.concatenate(
            [x_ref[:, (4 * group + k) * 256 : (4 * group + k + 1) * 256] for k in range(4)], axis=0
        )
        basis = v_ref[4 * group : 4 * group + 4].reshape(128, 256)
        coefs = lax.dot_general(block, basis, (((1,), (1,)), ((), ())), preferred_element_type=F32)
        wide_ref[pl.ds(64 * group, 64), :] = spread(coefs, group_mask, matrix)

    for level in range(5):
        first, after = LEVEL_ROW[level], LEVEL_ROW[level + 1]
        parents = []
        for g in range((after - first) // 2):
            total = None
            for child in (first + 2 * g, first + 2 * g + 1):
                term = apply(wide_ref[pl.ds(16 * child, 16), :], ef_ref[pl.ds(child, 1), :])
                total = term if total is None else total + term
            parents.append(fold(total))
        rows = 16 * len(parents)
        coefs = jnp.concatenate(parents, axis=0) if len(parents) > 1 else parents[0]
        wide_ref[pl.ds(16 * after, rows), :] = spread(coefs, first_group(rows), matrix)
    lift_ref[...] = fold(apply(wide_ref[pl.ds(16 * 62, 16), :], ef_ref[pl.ds(62, 1), :]))

    low_half = iota((8, 128), 1) < 64
    even = (iota((8, 128), 1) // 32) % 2 == 0
    prod_ref[pl.ds(504, 8), :] = jnp.zeros((8, 512), F32)

    @pl.loop(0, 63)
    def _(p):
        couple = b_ref[p].astype(F32)
        for quad in range(4):
            sums = [
                apply(couple, wide_ref[pl.ds(p * 16 + 4 * quad + k, 1), :]) for k in range(4)
            ]
            a0, a1, a2, a3 = sums[2], sums[1], sums[0], sums[3]
            w02 = jnp.where(low_half, a0, a2) + pltpu.roll(jnp.where(low_half, a2, a0), 64, 1)
            w13 = jnp.where(low_half, a1, a3) + pltpu.roll(jnp.where(low_half, a3, a1), 64, 1)
            w20 = pltpu.roll(w02, 64, 1)
            done = jnp.where(even, w20, w13) + pltpu.roll(jnp.where(even, w13, w02), 32, 1)
            prod_ref[pl.ds(p * 8, 8), pl.ds(128 * quad, 128)] = done

    table = lane_ref[...]
    pick = (iota((8, 768), 0) == table[1:2, :]).astype(F32)
    mine = (iota((63, 768), 0) == table[0:1, :]).astype(F32)
    offset = jnp.sum(dot((fd_ref[...] - me + 32).astype(F32), pick) * mine, axis=0, keepdims=True)
    slot = jnp.sum(dot(fs_ref[...].astype(F32), pick) * mine, axis=0, keepdims=True)
    target = table[2:3, :] * (offset.astype(jnp.int32) - 32) + slot.astype(jnp.int32) + table[3:4, :]

    def chosen(rows, start, lanes, high, low):
        hot = jnp.where(iota((rows, lanes), 0) == target[:, start : start + lanes], 1.0, 0.0)
        hot = hot.astype(BF16)
        return dot(hot, high) + dot(hot, low)

    def put(offset, tile, value):
        if offset == 0:
            own_ref[tile] = value
        else:
            send_ref[slot_of(offset) + tile] = value.astype(BF16)

    out = chosen(160, 0, 256, *halves(prod_ref[0:256, :]))
    for k in range(5):
        for half in range(2):
            for j in range(4):
                put(k - 2, 8 + 4 * half + j, out[k * 32 + half * 16 : k * 32 + half * 16 + 16, j * 128 : j * 128 + 128])
    out = chosen(144, 256, 128, *halves(prod_ref[256:384, :]))
    for k in range(9):
        for j in range(4):
            put(k - 4, 4 + j, out[k * 16 : k * 16 + 16, j * 128 : j * 128 + 128])
    part = jnp.concatenate([prod_ref[384:448, j * 256 : j * 256 + 256] for j in range(2)], axis=0)
    out = chosen(272, 384, 128, *halves(part))
    for k in range(17):
        for j in range(2):
            put(k - 8, 2 + j, out[k * 16 : k * 16 + 16, j * 128 : j * 128 + 128])
    part = jnp.concatenate([prod_ref[448:480, j * 128 : j * 128 + 128] for j in range(4)], axis=0)
    out = chosen(528, 512, 128, *halves(part))
    for k in range(33):
        put(k - 16, 1, out[k * 16 : k * 16 + 16, :])
    part = jnp.concatenate([prod_ref[480:512, j * 128 : j * 128 + 128] for j in range(4)], axis=0)
    out = chosen(1040, 640, 128, *halves(part))
    for k in range(65):
        put(k - 32, 0, out[k * 16 : k * 16 + 16, :])


def link_kernel(
    send_ref, own_ref, lift_ref, f_ref, x_ref, rr_ref, near_index, self_hbm, near_hbm,
    sum_ref, upper_ref, near_ref,
    far_ref, shock_ref, lifts_ref, pack_ref, self_v, near_v,
    far_send, far_recv, shock_send, shock_recv, in_send, in_recv, out_send, out_recv, load_sem,
):
    outer = lax.axis_index("outer")
    inner = lax.axis_index("inner")
    me = outer * 8 + inner

    def load(c, kind):
        source, target = (self_hbm, self_v) if kind == 0 else (near_hbm, near_v)
        return pltpu.make_async_copy(
            source.at[pl.ds(4 * c, 4)], target.at[pl.ds(4 * c, 4)], load_sem.at[kind, c]
        )

    def place(index):
        return (lax.div(index, 8), lax.rem(index, 8))

    barrier = pltpu.get_barrier_semaphore()

    @pl.loop(1, 33)
    def _(step):
        pl.semaphore_signal(barrier, inc=1, device_id=place(lax.rem(me + step, 128)), device_id_type=MESH)
        pl.semaphore_signal(barrier, inc=1, device_id=place(lax.rem(me + 128 - step, 128)), device_id_type=MESH)

    @pl.loop(5, 12)
    def _(step):
        pl.semaphore_signal(barrier, inc=1, device_id=(lax.rem(outer + step, 16), inner), device_id_type=MESH)

    for c in range(8):
        for kind in range(2):
            load(c, kind).start()
    for g in range(32):
        shock_ref[32 + g] = x_ref[:, 256 * g : 256 * g + 256]
    shock_ref[96] = jnp.zeros((16, 256), BF16)
    pl.semaphore_wait(barrier, 71)

    def lift_copy(k):
        return pltpu.make_async_remote_copy(
            src_ref=lift_ref,
            dst_ref=lifts_ref.at[inner],
            send_sem=in_send.at[k - 1],
            recv_sem=in_recv.at[k - 1],
            device_id=(outer, lax.rem(inner + k, 8)),
            device_id_type=MESH,
        )

    def pack_copy(k):
        return pltpu.make_async_remote_copy(
            src_ref=pack_ref,
            dst_ref=upper_ref.at[outer],
            send_sem=out_send.at[k - 1],
            recv_sem=out_recv.at[k - 1],
            device_id=(lax.rem(outer + k, 16), inner),
            device_id_type=MESH,
        )

    def shock_copy(k):
        return pltpu.make_async_remote_copy(
            src_ref=shock_ref.at[pl.ds(32, 32)],
            dst_ref=shock_ref.at[pl.ds(64 * k, 32)],
            send_sem=shock_send.at[k],
            recv_sem=shock_recv.at[k],
            device_id=place(lax.rem(me + (1 if k == 0 else 127), 128)),
            device_id_type=MESH,
        )

    def far_copy(number, index):
        near, far, tiles, base = CLASSES[number]
        count = far - near + 1
        offset = jnp.where(index < count, index - far, index - count + near)
        first = sum(2 * (c[1] - c[0] + 1) for c in CLASSES[:number])
        span = pl.ds(base + index * tiles, tiles)
        return pltpu.make_async_remote_copy(
            src_ref=send_ref.at[span],
            dst_ref=far_ref.at[span],
            send_sem=far_send.at[first + index],
            recv_sem=far_recv.at[first + index],
            device_id=place(lax.rem(me + offset + 128, 128)),
            device_id_type=MESH,
        )

    for k in range(1, 8):
        lift_copy(k).start()
    for number in range(5):
        near, far, _, _ = CLASSES[number]

        @pl.loop(0, 2 * (far - near + 1))
        def _(index, number=number):
            far_copy(number, index).start()

    for k in range(2):
        shock_copy(k).start()
    lifts_ref[inner] = lift_ref[...]

    matrix = rr_ref[...]
    for k in range(1, 8):
        lift_copy(k).wait_recv()
    sixth = [lifts_ref[2 * j] + lifts_ref[2 * j + 1] for j in range(4)]
    wide = spread(jnp.concatenate(sixth, axis=0), first_group(64), matrix)
    fifth = [
        fold(
            apply(wide[32 * j : 32 * j + 16], f_ref[2 * j : 2 * j + 1, :])
            + apply(wide[32 * j + 16 : 32 * j + 32], f_ref[2 * j + 1 : 2 * j + 2, :])
        )
        for j in range(2)
    ]
    wide = spread(jnp.concatenate(fifth, axis=0), first_group(32), matrix)
    fourth = fold(apply(wide[0:16], f_ref[4:5, :]) + apply(wide[16:32], f_ref[5:6, :]))
    group = iota((16, 128), 1) // 32
    pack_ref[:, 0:128] = jnp.where(
        group < 2, jnp.where(group == 0, sixth[0], sixth[1]), jnp.where(group == 2, sixth[2], sixth[3])
    )
    pack_ref[:, 128:256] = jnp.where(
        group < 2, jnp.where(group == 0, fifth[0], fifth[1]), jnp.where(group == 2, fourth, 0.0)
    )
    for k in range(1, 16):
        pack_copy(k).start()
    upper_ref[outer] = pack_ref[...]

    for k in range(2):
        shock_copy(k).wait_recv()
    for c in range(8):
        for kind in range(2):
            load(c, kind).wait()

        @pl.loop(4 * c, 4 * c + 4)
        def _(g):
            total = dot(shock_ref[32 + g], self_v[g])
            for j in range(3):
                total = total + dot(shock_ref[near_index[g * 3 + j]], near_v[g, j])
            near_ref[:, pl.ds(pl.multiple_of(g * 256, 256), 256)] = total

    sum_ref[...] = own_ref[...]
    for number in range(5):
        near, far, tiles, base = CLASSES[number]

        @pl.loop(0, 2 * (far - near + 1))
        def _(index, number=number, tiles=tiles, base=base):
            far_copy(number, index).wait_recv()
            for t in range(tiles):
                sum_ref[t] = sum_ref[t] + far_ref[base + index * tiles + t].astype(F32)

    for k in range(1, 16):
        pack_copy(k).wait_recv()
    for k in range(1, 8):
        lift_copy(k).wait_send()
    for k in range(1, 16):
        pack_copy(k).wait_send()
    for k in range(2):
        shock_copy(k).wait_send()
    for number in range(5):
        near, far, _, _ = CLASSES[number]

        @pl.loop(0, 2 * (far - near + 1))
        def _(index, number=number):
            far_copy(number, index).wait_send()


def down_kernel(
    sum_ref, upper_ref, near_ref, v_ref, e_ref, ut_ref, rr_ref, gather_ref, select_ref, partner_ref, uc_hbm,
    out_ref,
    ef_ref, uf_ref, couple_ref, wide4_ref, wide3_ref, wide2_ref, lhs_ref, wide56_ref, inject_ref, local_ref,
    high_ref, low_ref, sem,
):
    outer = lax.axis_index("outer")
    me = outer * 8 + lax.axis_index("inner")
    nodes = [lax.div(128 + me, 2 ** (7 - level)) for level in range(2, 7)]
    loads = [
        pltpu.make_async_copy(uc_hbm.at[nodes[k] - 4], couple_ref.at[k], sem.at[k]) for k in range(5)
    ]
    for copy in loads:
        copy.start()
    matrix = rr_ref[...]
    gather = gather_ref[...]
    ef_ref[pl.ds(0, 63), :] = e_ref[...].astype(F32)
    uf_ref[...] = ut_ref[...].astype(F32)

    mask = iota((256, 128), 1) // 32 == 2
    wide4_ref[...] = spread(upper_ref[:, :, 128:256].reshape(256, 128), mask, matrix).reshape(16, 16, 1024)

    def parents(wide_ref, count, first):
        made = []
        for g in range(count):
            total = apply(wide_ref[2 * g], uf_ref[pl.ds(first + 2 * g, 1), :])
            total = total + apply(wide_ref[2 * g + 1], uf_ref[pl.ds(first + 2 * g + 1, 1), :])
            made.append(fold(total))
        return spread(jnp.concatenate(made, axis=0), first_group(16 * count), matrix).reshape(count, 16, 1024)

    wide3_ref[...] = parents(wide4_ref, 8, 8)
    wide2_ref[...] = parents(wide3_ref, 4, 0)

    lane_group = iota((16, 128), 1) // 32
    for f in range(8):
        node = partner_ref[nodes[4] - 4, f] - 64
        piece = upper_ref[lax.div(node, 4), :, 0:128]
        lhs_ref[pl.ds(16 * f, 16), :] = jnp.where(lane_group == lax.rem(node, 4), piece, 0.0)
        node = partner_ref[nodes[3] - 4, f] - 32
        piece = upper_ref[lax.div(node, 2), :, 128:256]
        lhs_ref[pl.ds(128 + 16 * f, 16), :] = jnp.where(lane_group == lax.rem(node, 2), piece, 0.0)
    high, low = halves(lhs_ref[...])
    wide56_ref[...] = dot(jnp.concatenate([high, low], axis=1), matrix).reshape(16, 16, 1024)
    for copy in loads:
        copy.wait()
    fields = []
    for k in range(5):
        couple = couple_ref[k].astype(F32)
        total = None
        for f in range(8):
            if k == 4:
                wide = wide56_ref[f]
            elif k == 3:
                wide = wide56_ref[8 + f]
            else:
                base, ref = ((4, wide2_ref), (8, wide3_ref), (16, wide4_ref))[k]
                wide = ref[partner_ref[nodes[k] - 4, f] - base]
            term = apply(wide, couple[f : f + 1, :])
            total = term if total is None else total + term
        fields.append(fold(total))

    half_mask = [iota((8, 128), 0) == 4 * a + iota((8, 128), 1) // 32 for a in range(2)]

    def source(p, j, a):
        if p < 32:
            return sum_ref[8 + 4 * (p // 16) + 2 * j + a, p % 16 : p % 16 + 1, :]
        if p < 48:
            return sum_ref[4 + 2 * j + a, p - 32 : p - 31, :]
        if p < 56:
            return sum_ref[2 + a, j * 8 + p - 48 : j * 8 + p - 47, :]
        row = (2 * j + a) * 4
        if p < 60:
            return sum_ref[1, row + p - 56 : row + p - 55, :]
        return sum_ref[0, row + p - 60 : row + p - 59, :]

    for p in range(63):
        for j in range(2):
            for a in range(2):
                inject_ref[pl.ds(16 * p + 8 * j, 8), 128 * a : 128 * a + 128] = jnp.where(
                    half_mask[a], source(p, j, a), 0.0
                )
    high, low = halves(inject_ref[...])
    local_ref[...] = dot(high, select_ref[...]) + dot(low, select_ref[...])

    def turn(field, row):
        return jnp.concatenate([field * row[:, t * 128 : t * 128 + 128] for t in range(8)], axis=1)

    def step(field, row):
        high, low = halves(turn(field, row))
        both = dot(jnp.concatenate([high, low], axis=0), gather)
        return both[0:16] + both[16:32]

    down = fields[0]
    for k in range(1, 5):
        down = fields[k] + step(down, uf_ref[pl.ds(nodes[k] - 8, 1), :])
    current = local_ref[pl.ds(16 * 62, 16), :] + step(down, ef_ref[pl.ds(62, 1), :])
    for level in range(4, -1, -1):
        first, after = LEVEL_ROW[level], LEVEL_ROW[level + 1]
        for c in range(after - first):
            parent = current[16 * (c // 2) : 16 * (c // 2) + 16]
            high, low = halves(turn(parent, ef_ref[pl.ds(first + c, 1), :]))
            high_ref[pl.ds(16 * c, 16), :] = high
            low_ref[pl.ds(16 * c, 16), :] = low
        rows = 16 * (after - first)
        current = (
            local_ref[pl.ds(16 * first, rows), :]
            + dot(high_ref[pl.ds(0, rows), :], gather)
            + dot(low_ref[pl.ds(0, rows), :], gather)
        )

    group_mask = iota((64, 128), 1) // 32 == iota((64, 128), 0) // 16
    for group in range(8):
        high, low = halves(jnp.where(group_mask, current[64 * group : 64 * group + 64], 0.0))
        basis = v_ref[4 * group : 4 * group + 4].reshape(128, 256)
        both = dot(jnp.concatenate([high, low], axis=0), basis)
        both = both[0:64] + both[64:128]
        for k in range(4):
            lanes = pl.ds((4 * group + k) * 256, 256)
            out_ref[:, lanes] = near_ref[:, lanes] + both[16 * k : 16 * k + 16]


def local(
    shocks,
    leaf_basis,
    self_block,
    near_block,
    near_offset,
    near_count,
    local_transfer,
    local_coupling,
    far_device,
    far_slot,
    upper_transfer,
    upper_coupling,
    upper_partner,
):
    matrix = jnp.asarray(SPREAD, BF16)
    me = lax.axis_index("outer") * 8 + lax.axis_index("inner")
    near_index = jnp.arange(32, dtype=jnp.int32)[:, None] + near_offset + 32
    source = me * 32 - 32 + near_index
    live = jnp.arange(3, dtype=jnp.int32)[None, :] < near_count[:, None]
    live = live & (source >= 0) & (source < 4096)
    near_index = jnp.where(live, near_index, 96).reshape(96)
    shape = jax.ShapeDtypeStruct
    limit = 56 * 2**20
    send, own, lift, links = pl.pallas_call(
        up_kernel,
        out_shape=(
            shape((TILES, 16, 128), BF16),
            shape((16, 16, 128), F32),
            shape((16, 128), F32),
            shape((8, 1024), F32),
        ),
        in_specs=[VMEM] * 9,
        out_specs=(VMEM,) * 4,
        scratch_shapes=[
            pltpu.VMEM((64, 1024), F32),
            pltpu.VMEM((120, 1024), F32),
            pltpu.VMEM((1008, 1024), F32),
            pltpu.VMEM((512, 512), F32),
        ],
        compiler_params=pltpu.CompilerParams(vmem_limit_bytes=limit),
        name="up",
    )(
        shocks, leaf_basis, local_transfer, local_coupling, far_device, far_slot, upper_transfer, matrix,
        jnp.asarray(LANES),
    )
    sums, upper, near = pl.pallas_call(
        link_kernel,
        out_shape=(
            shape((16, 16, 128), F32),
            shape((16, 16, 256), F32),
            shape((16, 8192), F32),
        ),
        in_specs=[VMEM] * 6 + [SMEM] + [ANY] * 2,
        out_specs=(VMEM,) * 3,
        scratch_shapes=[
            pltpu.VMEM((TILES, 16, 128), BF16),
            pltpu.VMEM((97, 16, 256), BF16),
            pltpu.VMEM((8, 16, 128), F32),
            pltpu.VMEM((16, 256), F32),
            pltpu.VMEM((32, 256, 256), BF16),
            pltpu.VMEM((32, 3, 256, 256), BF16),
            pltpu.SemaphoreType.DMA((MESSAGES,)),
            pltpu.SemaphoreType.DMA((MESSAGES,)),
            pltpu.SemaphoreType.DMA((2,)),
            pltpu.SemaphoreType.DMA((2,)),
            pltpu.SemaphoreType.DMA((7,)),
            pltpu.SemaphoreType.DMA((7,)),
            pltpu.SemaphoreType.DMA((15,)),
            pltpu.SemaphoreType.DMA((15,)),
            pltpu.SemaphoreType.DMA((2, 8)),
        ],
        compiler_params=pltpu.CompilerParams(
            vmem_limit_bytes=limit, collective_id=0, has_side_effects=True
        ),
        name="link",
    )(send, own, lift, links, shocks, matrix, near_index, self_block, near_block)
    return pl.pallas_call(
        down_kernel,
        out_shape=shape((16, 8192), F32),
        in_specs=[VMEM] * 9 + [SMEM, ANY],
        out_specs=VMEM,
        scratch_shapes=[
            pltpu.VMEM((64, 1024), F32),
            pltpu.VMEM((120, 1024), F32),
            pltpu.VMEM((5, 8, 1024), BF16),
            pltpu.VMEM((16, 16, 1024), F32),
            pltpu.VMEM((8, 16, 1024), F32),
            pltpu.VMEM((4, 16, 1024), F32),
            pltpu.VMEM((256, 128), F32),
            pltpu.VMEM((16, 16, 1024), F32),
            pltpu.VMEM((1008, 256), F32),
            pltpu.VMEM((1008, 128), F32),
            pltpu.VMEM((512, 1024), BF16),
            pltpu.VMEM((512, 1024), BF16),
            pltpu.SemaphoreType.DMA((5,)),
        ],
        compiler_params=pltpu.CompilerParams(vmem_limit_bytes=limit),
        name="down",
    )(
        sums, upper, near, leaf_basis, local_transfer, upper_transfer, matrix, jnp.asarray(GATHER, BF16),
        jnp.asarray(SELECT, BF16), upper_partner, upper_coupling,
    )


def solution(mesh):
    both = ("outer", "inner")
    placed = (
        P(None, both),
        P(both, None, None),
        P(both, None, None),
        P(both, None, None, None),
        P(both, None),
        P(both),
        P(both, None),
        P(both, None, None),
        P(both, None),
        P(both, None),
        P(),
        P(),
        P(),
    )
    return jax.shard_map(
        local, mesh=mesh, in_specs=placed, out_specs=P(None, both), check_vma=False
    )
```

time: 587 us -> 69.9 us (0.12)
  the two profiles are of different devices: /device:TPU:1 before, /device:TPU:4 now
where the time goes in v1:
time: 69.9 us; the launch traced here: 69.6 us
  Pallas kernels  64.6 us (92%)
  local copies, waits for them, and re-layouts  4.29 us (6%)
    pallas_call x1, Pallas kernels, local(): pl.pallas_call(link_kernel, out_shape=(shape((16, 16, 128), F32), shape((...  36.4 us
    pallas_call x1, Pallas kernels, local(): pl.pallas_call(up_kernel, out_shape=(shape((TILES, 16, 128), BF16), shape...  19.8 us
    pallas_call x1, Pallas kernels, local(): pl.pallas_call(down_kernel, out_shape=shape((16, 8192), F32), in_specs=[V...  8.33 us
    unnamed x5, local copies, waits for them, and re-layouts  3.5 us

profile of v1, /device:TPU:4, one launch (start us, length us, event | category | flops | bytes accessed | tf_op | source)
XLA Modules:
  0.0 69.6 jit_solution(1331686851927424491)
XLA Ops:
  0.0 1.4 %copy.22.fd_ref = s32[63,8]{1,0:T(8,128)} copy(s32[63,8]{0,1:T(8,128)} %param.25) | data formatting | bytes 4032 | tf_op args[8]
  1.4 1.4 %copy.23.fs_ref = s32[63,8]{1,0:T(8,128)} copy(s32[63,8]{0,1:T(8,128)} %param.26) | data formatting | bytes 4032 | tf_op args[9]
  2.8 19.8 %up.1 = (bf16[192,16,128]{2,1,0:T(8,128)(2,1)}, f32[16,16,128]{2,1,0:T(8,128)}, f32[16,128]{1,0:T(8,128)}, f32[8,1024]{1,0:T(8,128)}) custom-call(bf16[16,8192]{1,0:T(8,128)(2,1)} %x_ref.3, bf16[32,32,256]{2,1,0:T(8,128)(2,1)} %v_ref.3, bf16[63,1024]{1,0:T(8,128)(2,1)} %e_ref.3, bf16[63,8,1024]{2,1,0:T(8,128)(2,1)} %b_ref.1, s32[63,8]{1,0:T(8,128)} %copy.22.fd_ref, ...), custom_call_target="tpu_custom_call" | custom-call | tf_op jit(solution)/shard_map/up/pallas_call | solution.py:499
  22.6 0.7 fusion.2
  23.3 0.1 copy.24
  23.4 0.7 %reshape.4.near_index = s32[96]{0:T(128)} reshape(s32[32,3]{1,0:T(8,128)S(1)} %copy.24) | data formatting | bytes 768 | tf_op jit(solution)/shard_map/reshape | solution.py:496
  24.1 0.0 copy-start
  24.1 36.4 %link.1 = (f32[16,16,128]{2,1,0:T(8,128)}, f32[16,16,256]{2,1,0:T(8,128)}, f32[16,8192]{1,0:T(8,128)}) custom-call(bf16[192,16,128]{2,1,0:T(8,128)(2,1)} %get-tuple-element.12.send_ref, f32[16,16,128]{2,1,0:T(8,128)} %get-tuple-element.13.own_ref, f32[16,128]{1,0:T(8,128)} %get-tuple-element.14.lift_ref, f32[8,1024]{1,0:T(8,128)} %get-tuple-element.15.f_ref, ...), custom_call_target="tpu_custom_call" | custom-call | tf_op jit(solution)/shard_map/link/pallas_call | solution.py:521
  60.5 0.0 copy-done
  60.5 0.7 %copy.25.partner_ref = s32[124,8]{1,0:T(8,128)} copy(s32[124,8]{0,1:T(8,128)S(1)} %copy-done) | data formatting | bytes 7936 | tf_op args[12]
  61.2 8.3 %down.1 = f32[16,8192]{1,0:T(8,128)} custom-call(f32[16,16,128]{2,1,0:T(8,128)} %get-tuple-element.16.sum_ref, f32[16,16,256]{2,1,0:T(8,128)} %get-tuple-element.17.upper_ref, f32[16,8192]{1,0:T(8,128)} %get-tuple-element.18.near_ref, bf16[32,32,256]{2,1,0:T(8,128)(2,1)} %v_ref.3, bf16[63,1024]{1,0:T(8,128)(2,1)} %e_ref.3, bf16[120,1024]{1,0:T(8,128)(2,1)} %ut_ref.3, ...), custom_call_target="tpu_custom_call" | custom-call | tf_op jit(solution)/shard_map/down/pallas_call | solution.py:552
Async XLA Ops:
  24.1 36.4 %copy-start = (s32[124,8]{0,1:T(8,128)S(1)}, s32[124,8]{0,1:T(8,128)}, u32[]{:S(2)}) copy-start(s32[124,8]{0,1:T(8,128)} %param.29) | copy-start | bytes 11908

commit v2 on v1

v2 whole, which is shorter than its diff:
```python
import jax
import jax.numpy as jnp
import numpy as np
from jax import lax
from jax.experimental import pallas as pl
from jax.experimental.pallas import tpu as pltpu
from jax.sharding import PartitionSpec as P

F32 = jnp.float32
BF16 = jnp.bfloat16
MESH = pl.DeviceIdType.MESH
VMEM = pl.BlockSpec(memory_space=pltpu.VMEM)
SMEM = pl.BlockSpec(memory_space=pltpu.SMEM)
ANY = pl.BlockSpec(memory_space=pl.ANY)

CLASSES = ((1, 2, 16, 0), (3, 4, 8, 64), (5, 8, 4, 96), (9, 16, 2, 128), (17, 32, 1, 160))
TILES = 192


def slot_of(offset):
    for near, far, tiles, base in CLASSES:
        if near <= abs(offset) <= far:
            count = far - near + 1
            place = offset + far if offset < 0 else offset - near + count
            return base + place * tiles
    return None


LEVEL_ROW = (0, 32, 48, 56, 60, 62, 63)


def lane_table():
    table = np.zeros((8, 768), np.int32)
    for lane in range(768):
        if lane < 256:
            item, part, scale, shift = lane, 0, 32, 64
        elif lane < 384:
            item, part, scale, shift = lane, 0, 16, 64 - 32
        elif lane < 512:
            item, part = 384 + (lane - 384) % 64, (lane - 384) // 64
            scale, shift = 16, 128 + 8 * part - 48
        elif lane < 640:
            item, part = 448 + (lane - 512) % 32, (lane - 512) // 32
            scale, shift = 16, 256 + 4 * part - 56
        else:
            item, part = 480 + (lane - 640) % 32, (lane - 640) // 32
            scale, shift = 16, 512 + 4 * part - 60
        if item >= 504:
            scale, shift = 0, -1000000
        table[0, lane], table[1, lane], table[2, lane], table[3, lane] = item // 8, item % 8, scale, shift
    return table


LANES = lane_table()

def iota(shape, dim):
    return lax.broadcasted_iota(jnp.int32, shape, dim)


def halves(x):
    high = x.astype(BF16)
    low = (x - high.astype(F32)).astype(BF16)
    return high, low


def dot(a, b):
    return jnp.dot(a, b, preferred_element_type=F32)


def spread(coefs, mask, matrix):
    high, low = halves(jnp.where(mask, coefs, 0.0))
    return dot(jnp.concatenate([high, low], axis=1), matrix)


def fold(x):
    x = x + pltpu.roll(x, 64, 1)
    return x + pltpu.roll(x, 32, 1)


def apply(wide, row):
    total = wide[:, 0:128] * row[:, 0:128]
    for t in range(1, 8):
        total = total + wide[:, t * 128 : t * 128 + 128] * row[:, t * 128 : t * 128 + 128]
    return total


def first_group(rows):
    return iota((rows, 128), 1) < 32


def kernel(
    x_ref, v_ref, e_ref, ut_ref, fd_ref, fs_ref, lane_ref, off_ref, count_ref, partner_ref,
    b_hbm, uc_hbm, self_hbm, near_hbm,
    out_ref,
    b_ref, self_v, near_v, couple_ref, ef_ref, uf_ref, wide_ref, prod_ref, spread_ref, gather_ref, select_ref,
    send_ref, far_ref, sum_ref, shock_ref, lift_ref, lifts_ref, pack_ref, upper_ref,
    index_v, index_s, node_ref, top_ref, wide56_ref,
    inject_ref, local_ref, high_ref, low_ref,
    load_sem, couple_sem, index_sem, far_send, far_recv, shock_send, shock_recv, in_send, in_recv,
    out_send, out_recv,
):
    outer = lax.axis_index("outer")
    inner = lax.axis_index("inner")
    me = outer * 8 + inner
    nodes = [lax.div(128 + me, 2 ** (7 - level)) for level in range(2, 7)]

    def place(index):
        return (lax.div(index, 8), lax.rem(index, 8))

    def load_basis():
        return pltpu.make_async_copy(b_hbm, b_ref.at[pl.ds(0, 63)], load_sem.at[2, 0])

    def load_upper(k):
        return pltpu.make_async_copy(uc_hbm.at[nodes[k] - 4], couple_ref.at[k], couple_sem.at[k])

    def load(c, kind):
        source, target = (self_hbm, self_v) if kind == 0 else (near_hbm, near_v)
        return pltpu.make_async_copy(
            source.at[pl.ds(4 * c, 4)], target.at[pl.ds(4 * c, 4)], load_sem.at[kind, c]
        )

    load_basis().start()
    for k in range(5):
        load_upper(k).start()
    for c in range(8):
        for kind in range(2):
            load(c, kind).start()

    barrier = pltpu.get_barrier_semaphore()

    @pl.loop(1, 33)
    def _(step):
        pl.semaphore_signal(barrier, inc=1, device_id=place(lax.rem(me + step, 128)), device_id_type=MESH)
        pl.semaphore_signal(barrier, inc=1, device_id=place(lax.rem(me + 128 - step, 128)), device_id_type=MESH)

    @pl.loop(5, 12)
    def _(step):
        pl.semaphore_signal(barrier, inc=1, device_id=(lax.rem(outer + step, 16), inner), device_id_type=MESH)

    unit = jnp.where(iota((32, 1024), 0) == iota((32, 1024), 1) // 32, 1.0, 0.0).astype(BF16)
    for k in range(8):
        spread_ref[32 * k : 32 * k + 32, :] = unit
    gather_ref[...] = jnp.where(iota((1024, 128), 0) // 32 == iota((1024, 128), 1) % 32, 1.0, 0.0).astype(BF16)
    unit = jnp.where(iota((32, 128), 0) == iota((32, 128), 1) % 32, 1.0, 0.0).astype(BF16)
    for k in range(8):
        select_ref[32 * k : 32 * k + 32, :] = unit

    near_row = iota((3, 32), 1) + off_ref[...] + 32
    source = me * 32 - 32 + near_row
    live = (iota((3, 32), 0) < count_ref[...]) & (source >= 0) & (source < 4096)
    index_v[...] = jnp.zeros((8, 128), jnp.int32)
    index_v[0:3, 0:32] = jnp.where(live, near_row, 96)
    index_copy = pltpu.make_async_copy(index_v, index_s, index_sem)
    index_copy.start()
    for g in range(32):
        shock_ref[32 + g] = x_ref[:, 256 * g : 256 * g + 256]
    shock_ref[96] = jnp.zeros((16, 256), BF16)
    ef_ref[pl.ds(0, 63), :] = e_ref[...].astype(F32)
    uf_ref[...] = ut_ref[...].astype(F32)
    matrix = spread_ref[...]

    group_mask = iota((64, 128), 1) // 32 == iota((64, 128), 0) // 16
    for group in range(8):
        block = shock_ref[32 + 4 * group : 36 + 4 * group].reshape(64, 256)
        basis = v_ref[4 * group : 4 * group + 4].reshape(128, 256)
        coefs = lax.dot_general(block, basis, (((1,), (1,)), ((), ())), preferred_element_type=F32)
        wide_ref[pl.ds(64 * group, 64), :] = spread(coefs, group_mask, matrix)

    for level in range(5):
        first, after = LEVEL_ROW[level], LEVEL_ROW[level + 1]
        parents = []
        for g in range((after - first) // 2):
            total = None
            for child in (first + 2 * g, first + 2 * g + 1):
                term = apply(wide_ref[pl.ds(16 * child, 16), :], ef_ref[pl.ds(child, 1), :])
                total = term if total is None else total + term
            parents.append(fold(total))
        rows = 16 * len(parents)
        coefs = jnp.concatenate(parents, axis=0) if len(parents) > 1 else parents[0]
        wide_ref[pl.ds(16 * after, rows), :] = spread(coefs, first_group(rows), matrix)
    lift_ref[...] = fold(apply(wide_ref[pl.ds(16 * 62, 16), :], ef_ref[pl.ds(62, 1), :]))

    def lift_copy(k):
        return pltpu.make_async_remote_copy(
            src_ref=lift_ref,
            dst_ref=lifts_ref.at[inner],
            send_sem=in_send,
            recv_sem=in_recv,
            device_id=(outer, lax.rem(inner + k, 8)),
            device_id_type=MESH,
        )

    def pack_copy(k):
        return pltpu.make_async_remote_copy(
            src_ref=pack_ref,
            dst_ref=upper_ref.at[outer],
            send_sem=out_send,
            recv_sem=out_recv,
            device_id=(lax.rem(outer + k, 16), inner),
            device_id_type=MESH,
        )

    def shock_copy(k):
        return pltpu.make_async_remote_copy(
            src_ref=shock_ref.at[pl.ds(32, 32)],
            dst_ref=shock_ref.at[pl.ds(64 * k, 32)],
            send_sem=shock_send.at[k],
            recv_sem=shock_recv.at[k],
            device_id=place(lax.rem(me + (1 if k == 0 else 127), 128)),
            device_id_type=MESH,
        )

    def far_start(number):
        near, far, tiles, base = CLASSES[number]
        count = far - near + 1

        @pl.loop(0, 2 * count)
        def _(index):
            offset = jnp.where(index < count, index - far, index - count + near)
            span = pl.ds(base + index * tiles, tiles)
            pltpu.make_async_remote_copy(
                src_ref=send_ref.at[span],
                dst_ref=far_ref.at[span],
                send_sem=far_send.at[number],
                recv_sem=far_recv.at[number],
                device_id=place(lax.rem(me + offset + 128, 128)),
                device_id_type=MESH,
            ).start()

    def wait_all(ref, sem):
        pltpu.make_async_copy(ref, ref, sem).wait()

    def far_part(ref, number):
        near, far, tiles, base = CLASSES[number]
        return ref.at[pl.ds(base, 2 * (far - near + 1) * tiles)]

    pl.semaphore_wait(barrier, 71)
    for k in range(1, 8):
        lift_copy(k).start()
    for k in range(2):
        shock_copy(k).start()
    lifts_ref[inner] = lift_ref[...]

    table = lane_ref[...]
    pick = (iota((8, 768), 0) == table[1:2, :]).astype(F32)
    mine = (iota((63, 768), 0) == table[0:1, :]).astype(F32)
    offset = jnp.sum(dot((fd_ref[...] - me + 32).astype(F32), mine) * pick, axis=0, keepdims=True)
    slot = jnp.sum(dot(fs_ref[...].astype(F32), mine) * pick, axis=0, keepdims=True)
    target = table[2:3, :] * (offset.astype(jnp.int32) - 32) + slot.astype(jnp.int32) + table[3:4, :]

    low_half = iota((8, 128), 1) < 64
    even = (iota((8, 128), 1) // 32) % 2 == 0

    def couple(start, stop):
        @pl.loop(start, stop, unroll=8)
        def _(p):
            blocks = b_ref[p].astype(F32)
            for quad in range(4):
                sums = [apply(blocks, wide_ref[pl.ds(p * 16 + 4 * quad + k, 1), :]) for k in range(4)]
                a0, a1, a2, a3 = sums[2], sums[1], sums[0], sums[3]
                w02 = jnp.where(low_half, a0, a2) + pltpu.roll(jnp.where(low_half, a2, a0), 64, 1)
                w13 = jnp.where(low_half, a1, a3) + pltpu.roll(jnp.where(low_half, a3, a1), 64, 1)
                w20 = pltpu.roll(w02, 64, 1)
                done = jnp.where(even, w20, w13) + pltpu.roll(jnp.where(even, w13, w02), 32, 1)
                prod_ref[pl.ds(p * 8, 8), pl.ds(128 * quad, 128)] = done

    def chosen(rows, start, lanes, high, low):
        hot = jnp.where(iota((rows, lanes), 0) == target[:, start : start + lanes], 1.0, 0.0)
        hot = hot.astype(BF16)
        return dot(hot, high) + dot(hot, low)

    def put(offset, tile, value):
        if offset == 0:
            sum_ref[tile] = value
        else:
            send_ref[slot_of(offset) + tile] = value.astype(BF16)

    wide_ref[1008:1024, :] = jnp.zeros((16, 1024), F32)
    load_basis().wait()
    b_ref[63] = jnp.zeros((8, 1024), BF16)
    couple(32, 64)
    part = jnp.concatenate([prod_ref[480:512, j * 128 : j * 128 + 128] for j in range(4)], axis=0)
    out = chosen(1040, 640, 128, *halves(part))
    for k in range(65):
        put(k - 32, 0, out[k * 16 : k * 16 + 16, :])
    far_start(4)
    part = jnp.concatenate([prod_ref[448:480, j * 128 : j * 128 + 128] for j in range(4)], axis=0)
    out = chosen(528, 512, 128, *halves(part))
    for k in range(33):
        put(k - 16, 1, out[k * 16 : k * 16 + 16, :])
    far_start(3)
    part = jnp.concatenate([prod_ref[384:448, j * 256 : j * 256 + 256] for j in range(2)], axis=0)
    out = chosen(272, 384, 128, *halves(part))
    for k in range(17):
        for j in range(2):
            put(k - 8, 2 + j, out[k * 16 : k * 16 + 16, j * 128 : j * 128 + 128])
    far_start(2)
    out = chosen(144, 256, 128, *halves(prod_ref[256:384, :]))
    for k in range(9):
        for j in range(4):
            put(k - 4, 4 + j, out[k * 16 : k * 16 + 16, j * 128 : j * 128 + 128])
    far_start(1)

    wait_all(lifts_ref.at[pl.ds(0, 7)], in_recv)
    sixth = [lifts_ref[2 * j] + lifts_ref[2 * j + 1] for j in range(4)]
    wide = spread(jnp.concatenate(sixth, axis=0), first_group(64), matrix)

    def link(first, k):
        return uf_ref[pl.ds(first + k, 1), :]

    fifth = [
        fold(
            apply(wide[32 * j : 32 * j + 16], link(56 + 4 * outer, 2 * j))
            + apply(wide[32 * j + 16 : 32 * j + 32], link(56 + 4 * outer, 2 * j + 1))
        )
        for j in range(2)
    ]
    wide = spread(jnp.concatenate(fifth, axis=0), first_group(32), matrix)
    fourth = fold(apply(wide[0:16], link(24 + 2 * outer, 0)) + apply(wide[16:32], link(24 + 2 * outer, 1)))
    group = iota((16, 128), 1) // 32
    pack_ref[:, 0:128] = jnp.where(
        group < 2, jnp.where(group == 0, sixth[0], sixth[1]), jnp.where(group == 2, sixth[2], sixth[3])
    )
    pack_ref[:, 128:256] = jnp.where(
        group < 2, jnp.where(group == 0, fifth[0], fifth[1]), jnp.where(group == 2, fourth, 0.0)
    )
    for k in range(1, 16):
        pack_copy(k).start()
    upper_ref[outer] = pack_ref[...]

    couple(0, 32)
    out = chosen(160, 0, 256, *halves(prod_ref[0:256, :]))
    for k in range(5):
        for half in range(2):
            for j in range(4):
                row = k * 32 + half * 16
                put(k - 2, 8 + 4 * half + j, out[row : row + 16, j * 128 : j * 128 + 128])
    far_start(0)

    index_copy.wait()
    for k in range(2):
        shock_copy(k).wait_recv()
    for c in range(8):
        for kind in range(2):
            load(c, kind).wait()

        @pl.loop(4 * c, 4 * c + 4, unroll=2)
        def _(g):
            total = dot(shock_ref[32 + g], self_v[g])
            for j in range(3):
                total = total + dot(shock_ref[index_s[j, g]], near_v[g, j])
            out_ref[:, pl.ds(pl.multiple_of(g * 256, 256), 256)] = total

    wait_all(upper_ref.at[pl.ds(0, 15)], out_recv)
    mask = iota((256, 128), 1) // 32 == 2
    node_ref[0] = jnp.zeros((16, 128), F32)
    top_ref[0] = jnp.zeros((16, 1024), F32)
    top_ref[16:32] = spread(upper_ref[:, :, 128:256].reshape(256, 128), mask, matrix).reshape(16, 16, 1024)
    for k in range(16):
        for j in range(4):
            node_ref[64 + 4 * k + j] = jnp.where(group == j, upper_ref[k, :, 0:128], 0.0)
        for j in range(2):
            node_ref[32 + 2 * k + j] = jnp.where(group == j, upper_ref[k, :, 128:256], 0.0)

    def parents(count):
        made = []
        for g in range(count, 2 * count):
            total = apply(top_ref[2 * g], uf_ref[pl.ds(2 * g - 8, 1), :])
            total = total + apply(top_ref[2 * g + 1], uf_ref[pl.ds(2 * g - 7, 1), :])
            made.append(fold(total))
        wide = spread(jnp.concatenate(made, axis=0), first_group(16 * count), matrix)
        top_ref[count : 2 * count] = wide.reshape(count, 16, 1024)

    parents(8)
    parents(4)

    rows = [node_ref[partner_ref[f, nodes[k] - 4]] for k in (4, 3) for f in range(8)]
    high, low = halves(jnp.concatenate(rows, axis=0))
    wide56_ref[...] = dot(jnp.concatenate([high, low], axis=1), matrix).reshape(16, 16, 1024)
    fields = []
    for k in range(5):
        load_upper(k).wait()
        blocks = couple_ref[k].astype(F32)
        total = None
        for f in range(8):
            if k == 4:
                wide = wide56_ref[f]
            elif k == 3:
                wide = wide56_ref[8 + f]
            else:
                wide = top_ref[partner_ref[f, nodes[k] - 4]]
            term = apply(wide, blocks[f : f + 1, :])
            total = term if total is None else total + term
        fields.append(fold(total))

    gather = gather_ref[...]

    def turn(field, row):
        return jnp.concatenate([field * row[:, t * 128 : t * 128 + 128] for t in range(8)], axis=1)

    def step(field, row):
        high, low = halves(turn(field, row))
        both = dot(jnp.concatenate([high, low], axis=0), gather)
        return both[0:16] + both[16:32]

    down = fields[0]
    for k in range(1, 5):
        down = fields[k] + step(down, uf_ref[pl.ds(nodes[k] - 8, 1), :])
    current = step(down, ef_ref[pl.ds(62, 1), :])

    for number in (4, 3, 2, 1, 0):
        near, far, tiles, base = CLASSES[number]
        count = 2 * (far - near + 1)
        wait_all(far_part(far_ref, number), far_recv.at[number])
        for t in range(tiles):
            total = sum_ref[t]
            for k in range(count):
                total = total + far_ref[base + k * tiles + t].astype(F32)
            sum_ref[t] = total

    half_mask = [iota((8, 128), 0) == 4 * a + iota((8, 128), 1) // 32 for a in range(2)]

    def source_row(p, j, a):
        if p < 32:
            return sum_ref[8 + 4 * (p // 16) + 2 * j + a, p % 16 : p % 16 + 1, :]
        if p < 48:
            return sum_ref[4 + 2 * j + a, p - 32 : p - 31, :]
        if p < 56:
            return sum_ref[2 + a, j * 8 + p - 48 : j * 8 + p - 47, :]
        row = (2 * j + a) * 4
        if p < 60:
            return sum_ref[1, row + p - 56 : row + p - 55, :]
        return sum_ref[0, row + p - 60 : row + p - 59, :]

    for p in range(63):
        for j in range(2):
            for a in range(2):
                inject_ref[pl.ds(16 * p + 8 * j, 8), 128 * a : 128 * a + 128] = jnp.where(
                    half_mask[a], source_row(p, j, a), 0.0
                )
    high, low = halves(inject_ref[...])
    local_ref[...] = dot(high, select_ref[...]) + dot(low, select_ref[...])

    current = current + local_ref[pl.ds(16 * 62, 16), :]
    for level in range(4, -1, -1):
        first, after = LEVEL_ROW[level], LEVEL_ROW[level + 1]
        for c in range(after - first):
            parent = current[16 * (c // 2) : 16 * (c // 2) + 16]
            high, low = halves(turn(parent, ef_ref[pl.ds(first + c, 1), :]))
            high_ref[pl.ds(16 * c, 16), :] = high
            low_ref[pl.ds(16 * c, 16), :] = low
        rows = 16 * (after - first)
        current = (
            local_ref[pl.ds(16 * first, rows), :]
            + dot(high_ref[pl.ds(0, rows), :], gather)
            + dot(low_ref[pl.ds(0, rows), :], gather)
        )

    for group in range(8):
        high, low = halves(jnp.where(group_mask, current[64 * group : 64 * group + 64], 0.0))
        basis = v_ref[4 * group : 4 * group + 4].reshape(128, 256)
        both = dot(jnp.concatenate([high, low], axis=0), basis)
        both = both[0:64] + both[64:128]
        for k in range(4):
            lanes = pl.ds((4 * group + k) * 256, 256)
            out_ref[:, lanes] = out_ref[:, lanes] + both[16 * k : 16 * k + 16]

    wait_all(lifts_ref.at[pl.ds(0, 7)], in_send)
    wait_all(upper_ref.at[pl.ds(0, 15)], out_send)
    for k in range(2):
        shock_copy(k).wait_send()
    for number in range(5):
        wait_all(far_part(send_ref, number), far_send.at[number])


def local(
    shocks,
    leaf_basis,
    self_block,
    near_block,
    near_offset,
    near_count,
    local_transfer,
    local_coupling,
    far_device,
    far_slot,
    upper_transfer,
    upper_coupling,
    upper_partner,
):
    return pl.pallas_call(
        kernel,
        out_shape=jax.ShapeDtypeStruct((16, 8192), F32),
        in_specs=[VMEM] * 9 + [SMEM] + [ANY] * 4,
        out_specs=VMEM,
        scratch_shapes=[
            pltpu.VMEM((64, 8, 1024), BF16),
            pltpu.VMEM((32, 256, 256), BF16),
            pltpu.VMEM((32, 3, 256, 256), BF16),
            pltpu.VMEM((5, 8, 1024), BF16),
            pltpu.VMEM((64, 1024), F32),
            pltpu.VMEM((120, 1024), F32),
            pltpu.VMEM((1024, 1024), F32),
            pltpu.VMEM((512, 512), F32),
            pltpu.VMEM((256, 1024), BF16),
            pltpu.VMEM((1024, 128), BF16),
            pltpu.VMEM((256, 128), BF16),
            pltpu.VMEM((TILES, 16, 128), BF16),
            pltpu.VMEM((TILES, 16, 128), BF16),
            pltpu.VMEM((16, 16, 128), F32),
            pltpu.VMEM((97, 16, 256), BF16),
            pltpu.VMEM((16, 128), F32),
            pltpu.VMEM((8, 16, 128), F32),
            pltpu.VMEM((16, 256), F32),
            pltpu.VMEM((16, 16, 256), F32),
            pltpu.VMEM((8, 128), jnp.int32),
            pltpu.SMEM((8, 128), jnp.int32),
            pltpu.VMEM((128, 16, 128), F32),
            pltpu.VMEM((32, 16, 1024), F32),
            pltpu.VMEM((16, 16, 1024), F32),
            pltpu.VMEM((1008, 256), F32),
            pltpu.VMEM((1008, 128), F32),
            pltpu.VMEM((512, 1024), BF16),
            pltpu.VMEM((512, 1024), BF16),
            pltpu.SemaphoreType.DMA((3, 8)),
            pltpu.SemaphoreType.DMA((5,)),
            pltpu.SemaphoreType.DMA,
            pltpu.SemaphoreType.DMA((5,)),
            pltpu.SemaphoreType.DMA((5,)),
            pltpu.SemaphoreType.DMA((2,)),
            pltpu.SemaphoreType.DMA((2,)),
            pltpu.SemaphoreType.DMA,
            pltpu.SemaphoreType.DMA,
            pltpu.SemaphoreType.DMA,
            pltpu.SemaphoreType.DMA,
        ],
        compiler_params=pltpu.CompilerParams(
            vmem_limit_bytes=56 * 2**20, collective_id=0, has_side_effects=True
        ),
        name="whole",
    )(
        shocks, leaf_basis, local_transfer, upper_transfer, far_device.T, far_slot.T, jnp.asarray(LANES),
        near_offset.T, near_count.reshape(1, 32), upper_partner.T, local_coupling, upper_coupling,
        self_block, near_block,
    )


def solution(mesh):
    both = ("outer", "inner")
    placed = (
        P(None, both),
        P(both, None, None),
        P(both, None, None),
        P(both, None, None, None),
        P(both, None),
        P(both),
        P(both, None),
        P(both, None, None),
        P(both, None),
        P(both, None),
        P(),
        P(),
        P(),
    )
    return jax.shard_map(
        local, mesh=mesh, in_specs=placed, out_specs=P(None, both), check_vma=False
    )
```

time: 69.9 us -> 38.7 us (0.55)
  the two profiles are of different devices: /device:TPU:4 before, /device:TPU:1 now
where the time goes in v2:
time: 38.7 us; the launch traced here: 38.6 us
  Pallas kernels  36.7 us (95%)
  local copies, waits for them, and re-layouts  1.87 us (5%)
    pallas_call x1, Pallas kernels, local(): pl.pallas_call(kernel, out_shape=jax.ShapeDtypeStruct((16, 8192), F32), i...  36.7 us
    unnamed x1, local copies, waits for them, and re-layouts  1.87 us

profile of v2, /device:TPU:1, one launch (start us, length us, event | category | flops | bytes accessed | tf_op | source)
XLA Modules:
  0.0 38.6 jit_solution(12320819907212667507)
XLA Ops:
  0.0 36.7 %whole.1 = f32[16,8192]{1,0:T(8,128)} custom-call(bf16[16,8192]{1,0:T(8,128)(2,1)} %x_ref.1, bf16[32,32,256]{2,1,0:T(8,128)(2,1)} %v_ref.1, bf16[63,1024]{1,0:T(8,128)(2,1)} %e_ref.1, bf16[120,1024]{1,0:T(8,128)(2,1)} %ut_ref.1, s32[8,63]{1,0:T(8,128)} %bitcast.5, s32[8,63]{1,0:T(8,128)} %bitcast.6, s32[8,768]{1,0:T(8,128)} %constant.2.clone.lane_ref, ...), custom_call_target="tpu_custom_call" | custom-call | tf_op jit(solution)/shard_map/whole/pallas_call | solution.py:491
  36.7 1.9 %copy.16 = f32[16,8192]{1,0:T(8,128)} copy(f32[16,8192]{1,0:T(8,128)} %whole.1) | data formatting | bytes 1048576

commit v3 on v2

--- a/solution.py
+++ b/solution.py
@@ -279,6 +279,33 @@
     load_basis().wait()
     b_ref[63] = jnp.zeros((8, 1024), BF16)
     couple(32, 64)
+    wait_all(lifts_ref.at[pl.ds(0, 7)], in_recv)
+    sixth = [lifts_ref[2 * j] + lifts_ref[2 * j + 1] for j in range(4)]
+    wide = spread(jnp.concatenate(sixth, axis=0), first_group(64), matrix)
+
+    def link(first, k):
+        return uf_ref[pl.ds(first + k, 1), :]
+
+    fifth = [
+        fold(
+            apply(wide[32 * j : 32 * j + 16], link(56 + 4 * outer, 2 * j))
+            + apply(wide[32 * j + 16 : 32 * j + 32], link(56 + 4 * outer, 2 * j + 1))
+        )
+        for j in range(2)
+    ]
+    wide = spread(jnp.concatenate(fifth, axis=0), first_group(32), matrix)
+    fourth = fold(apply(wide[0:16], link(24 + 2 * outer, 0)) + apply(wide[16:32], link(24 + 2 * outer, 1)))
+    group = iota((16, 128), 1) // 32
+    pack_ref[:, 0:128] = jnp.where(
+        group < 2, jnp.where(group == 0, sixth[0], sixth[1]), jnp.where(group == 2, sixth[2], sixth[3])
+    ).astype(BF16)
+    pack_ref[:, 128:256] = jnp.where(
+        group < 2, jnp.where(group == 0, fifth[0], fifth[1]), jnp.where(group == 2, fourth, 0.0)
+    ).astype(BF16)
+    for k in range(1, 16):
+        pack_copy(k).start()
+    upper_ref[outer] = pack_ref[...]
+
     part = jnp.concatenate([prod_ref[480:512, j * 128 : j * 128 + 128] for j in range(4)], axis=0)
     out = chosen(1040, 640, 128, *halves(part))
     for k in range(65):
@@ -301,33 +328,6 @@
             put(k - 4, 4 + j, out[k * 16 : k * 16 + 16, j * 128 : j * 128 + 128])
     far_start(1)
 
-    wait_all(lifts_ref.at[pl.ds(0, 7)], in_recv)
-    sixth = [lifts_ref[2 * j] + lifts_ref[2 * j + 1] for j in range(4)]
-    wide = spread(jnp.concatenate(sixth, axis=0), first_group(64), matrix)
-
-    def link(first, k):
-        return uf_ref[pl.ds(first + k, 1), :]
-
-    fifth = [
-        fold(
-            apply(wide[32 * j : 32 * j + 16], link(56 + 4 * outer, 2 * j))
-            + apply(wide[32 * j + 16 : 32 * j + 32], link(56 + 4 * outer, 2 * j + 1))
-        )
-        for j in range(2)
-    ]
-    wide = spread(jnp.concatenate(fifth, axis=0), first_group(32), matrix)
-    fourth = fold(apply(wide[0:16], link(24 + 2 * outer, 0)) + apply(wide[16:32], link(24 + 2 * outer, 1)))
-    group = iota((16, 128), 1) // 32
-    pack_ref[:, 0:128] = jnp.where(
-        group < 2, jnp.where(group == 0, sixth[0], sixth[1]), jnp.where(group == 2, sixth[2], sixth[3])
-    )
-    pack_ref[:, 128:256] = jnp.where(
-        group < 2, jnp.where(group == 0, fifth[0], fifth[1]), jnp.where(group == 2, fourth, 0.0)
-    )
-    for k in range(1, 16):
-        pack_copy(k).start()
-    upper_ref[outer] = pack_ref[...]
-
     couple(0, 32)
     out = chosen(160, 0, 256, *halves(prod_ref[0:256, :]))
     for k in range(5):
@@ -353,14 +353,15 @@
 
     wait_all(upper_ref.at[pl.ds(0, 15)], out_recv)
     mask = iota((256, 128), 1) // 32 == 2
-    node_ref[0] = jnp.zeros((16, 128), F32)
+    node_ref[0] = jnp.zeros((16, 128), BF16)
     top_ref[0] = jnp.zeros((16, 1024), F32)
-    top_ref[16:32] = spread(upper_ref[:, :, 128:256].reshape(256, 128), mask, matrix).reshape(16, 16, 1024)
+    coefs = jnp.where(mask, upper_ref[:, :, 128:256].reshape(256, 128).astype(F32), 0.0).astype(BF16)
+    top_ref[16:32] = dot(coefs, spread_ref[0:128, :]).reshape(16, 16, 1024)
     for k in range(16):
         for j in range(4):
-            node_ref[64 + 4 * k + j] = jnp.where(group == j, upper_ref[k, :, 0:128], 0.0)
+            node_ref[64 + 4 * k + j] = jnp.where(group == j, upper_ref[k, :, 0:128].astype(F32), 0.0).astype(BF16)
         for j in range(2):
-            node_ref[32 + 2 * k + j] = jnp.where(group == j, upper_ref[k, :, 128:256], 0.0)
+            node_ref[32 + 2 * k + j] = jnp.where(group == j, upper_ref[k, :, 128:256].astype(F32), 0.0).astype(BF16)
 
     def parents(count):
         made = []
@@ -375,8 +376,7 @@
     parents(4)
 
     rows = [node_ref[partner_ref[f, nodes[k] - 4]] for k in (4, 3) for f in range(8)]
-    high, low = halves(jnp.concatenate(rows, axis=0))
-    wide56_ref[...] = dot(jnp.concatenate([high, low], axis=1), matrix).reshape(16, 16, 1024)
+    wide56_ref[...] = dot(jnp.concatenate(rows, axis=0), spread_ref[0:128, :]).reshape(16, 16, 1024)
     fields = []
     for k in range(5):
         load_upper(k).wait()
@@ -511,11 +511,11 @@
             pltpu.VMEM((97, 16, 256), BF16),
             pltpu.VMEM((16, 128), F32),
             pltpu.VMEM((8, 16, 128), F32),
-            pltpu.VMEM((16, 256), F32),
-            pltpu.VMEM((16, 16, 256), F32),
+            pltpu.VMEM((16, 256), BF16),
+            pltpu.VMEM((16, 16, 256), BF16),
             pltpu.VMEM((8, 128), jnp.int32),
             pltpu.SMEM((8, 128), jnp.int32),
-            pltpu.VMEM((128, 16, 128), F32),
+            pltpu.VMEM((128, 16, 128), BF16),
             pltpu.VMEM((32, 16, 1024), F32),
             pltpu.VMEM((16, 16, 1024), F32),
             pltpu.VMEM((1008, 256), F32),

time: 38.7 us -> 35.8 us (0.925)
  Pallas kernels: 36.7 us -> 33.8 us
    pallas_call x1, Pallas kernels: 36.7 us -> 33.8 us  [local(): pl.pallas_call(kernel, out_shape=jax.ShapeDtypeStruct((16, 8192), F32), i...]
where the time goes in v3:
time: 35.8 us; the launch traced here: 35.7 us
  Pallas kernels  33.8 us (94%)
  local copies, waits for them, and re-layouts  1.87 us (5%)
    pallas_call x1, Pallas kernels, local(): pl.pallas_call(kernel, out_shape=jax.ShapeDtypeStruct((16, 8192), F32), i...  33.8 us
    unnamed x1, local copies, waits for them, and re-layouts  1.87 us

profile of v3, /device:TPU:1, one launch (start us, length us, event | category | flops | bytes accessed | tf_op | source)
XLA Modules:
  0.0 35.7 jit_solution(308895877538997888)
XLA Ops:
  0.0 33.8 %whole.1 = f32[16,8192]{1,0:T(8,128)} custom-call(bf16[16,8192]{1,0:T(8,128)(2,1)} %x_ref.1, bf16[32,32,256]{2,1,0:T(8,128)(2,1)} %v_ref.1, bf16[63,1024]{1,0:T(8,128)(2,1)} %e_ref.1, bf16[120,1024]{1,0:T(8,128)(2,1)} %ut_ref.1, s32[8,63]{1,0:T(8,128)} %bitcast.5, s32[8,63]{1,0:T(8,128)} %bitcast.6, s32[8,768]{1,0:T(8,128)} %constant.2.clone.lane_ref, ...), custom_call_target="tpu_custom_call" | custom-call | tf_op jit(solution)/shard_map/whole/pallas_call | solution.py:491
  33.8 1.9 %copy.16 = f32[16,8192]{1,0:T(8,128)} copy(f32[16,8192]{1,0:T(8,128)} %whole.1) | data formatting | bytes 1048576

commit v4 on v3

--- a/solution.py
+++ b/solution.py
@@ -95,7 +95,7 @@
     b_ref, self_v, near_v, couple_ref, ef_ref, uf_ref, wide_ref, prod_ref, spread_ref, gather_ref, select_ref,
     send_ref, far_ref, sum_ref, shock_ref, lift_ref, lifts_ref, pack_ref, upper_ref,
     index_v, index_s, node_ref, top_ref, wide56_ref,
-    inject_ref, local_ref, high_ref, low_ref,
+    inject_ref, local_ref, high_ref, low_ref, near_ref, stack_ref,
     load_sem, couple_sem, index_sem, far_send, far_recv, shock_send, shock_recv, in_send, in_recv,
     out_send, out_recv,
 ):
@@ -119,23 +119,23 @@
             source.at[pl.ds(4 * c, 4)], target.at[pl.ds(4 * c, 4)], load_sem.at[kind, c]
         )
 
+    barrier = pltpu.get_barrier_semaphore()
+
+    @pl.loop(1, 33)
+    def _(step):
+        pl.semaphore_signal(barrier, inc=1, device_id=place(lax.rem(me + step, 128)), device_id_type=MESH)
+        pl.semaphore_signal(barrier, inc=1, device_id=place(lax.rem(me + 128 - step, 128)), device_id_type=MESH)
+
+    @pl.loop(5, 12)
+    def _(step):
+        pl.semaphore_signal(barrier, inc=1, device_id=(lax.rem(outer + step, 16), inner), device_id_type=MESH)
+
     load_basis().start()
     for k in range(5):
         load_upper(k).start()
     for c in range(8):
         for kind in range(2):
             load(c, kind).start()
-
-    barrier = pltpu.get_barrier_semaphore()
-
-    @pl.loop(1, 33)
-    def _(step):
-        pl.semaphore_signal(barrier, inc=1, device_id=place(lax.rem(me + step, 128)), device_id_type=MESH)
-        pl.semaphore_signal(barrier, inc=1, device_id=place(lax.rem(me + 128 - step, 128)), device_id_type=MESH)
-
-    @pl.loop(5, 12)
-    def _(step):
-        pl.semaphore_signal(barrier, inc=1, device_id=(lax.rem(outer + step, 16), inner), device_id_type=MESH)
 
     unit = jnp.where(iota((32, 1024), 0) == iota((32, 1024), 1) // 32, 1.0, 0.0).astype(BF16)
     for k in range(8):
@@ -337,6 +337,15 @@
                 put(k - 2, 8 + 4 * half + j, out[row : row + 16, j * 128 : j * 128 + 128])
     far_start(0)
 
+    spot = iota((32, 1024), 1) // 32 == iota((32, 1024), 0)
+    unit = jnp.where(iota((1024, 128), 0) % 32 == iota((1024, 128), 1) % 32, 1.0, 0.0).astype(BF16)
+    parent_mask = iota((256, 128), 1) // 32 == iota((256, 128), 0) // 64
+    for octet in range(7):
+        for k in range(8):
+            row = ef_ref[pl.ds(8 * octet + k, 1), :]
+            high_ref[pl.ds(32 * k, 32), :] = jnp.where(spot, row, 0.0).astype(BF16)
+        stack_ref[octet] = jnp.where(parent_mask, dot(high_ref[pl.ds(0, 256), :], unit), 0.0).astype(BF16)
+
     index_copy.wait()
     for k in range(2):
         shock_copy(k).wait_recv()
@@ -349,7 +358,7 @@
             total = dot(shock_ref[32 + g], self_v[g])
             for j in range(3):
                 total = total + dot(shock_ref[index_s[j, g]], near_v[g, j])
-            out_ref[:, pl.ds(pl.multiple_of(g * 256, 256), 256)] = total
+            near_ref[g] = total
 
     wait_all(upper_ref.at[pl.ds(0, 15)], out_recv)
     mask = iota((256, 128), 1) // 32 == 2
@@ -442,7 +451,7 @@
     local_ref[...] = dot(high, select_ref[...]) + dot(low, select_ref[...])
 
     current = current + local_ref[pl.ds(16 * 62, 16), :]
-    for level in range(4, -1, -1):
+    for level in range(4, 2, -1):
         first, after = LEVEL_ROW[level], LEVEL_ROW[level + 1]
         for c in range(after - first):
             parent = current[16 * (c // 2) : 16 * (c // 2) + 16]
@@ -456,14 +465,36 @@
             + dot(low_ref[pl.ds(0, rows), :], gather)
         )
 
-    for group in range(8):
-        high, low = halves(jnp.where(group_mask, current[64 * group : 64 * group + 64], 0.0))
-        basis = v_ref[4 * group : 4 * group + 4].reshape(128, 256)
-        both = dot(jnp.concatenate([high, low], axis=0), basis)
-        both = both[0:64] + both[64:128]
+    def side_by_side(ref_rows):
+        low_pair = jnp.where(group == 0, ref_rows[0:16], ref_rows[16:32])
+        high_pair = jnp.where(group == 2, ref_rows[32:48], ref_rows[48:64])
+        return jnp.where(group < 2, low_pair, high_pair)
+
+    def children(field, octet):
+        high, low = halves(field)
+        both = lax.dot_general(
+            jnp.concatenate([high, low], axis=0),
+            stack_ref[octet],
+            (((1,), (1,)), ((), ())),
+            preferred_element_type=F32,
+        )
+        both = both[0:16] + both[16:32]
+        return [
+            both[:, 128 * half : 128 * half + 128]
+            + side_by_side(local_ref[pl.ds(16 * (8 * octet + 4 * half), 64), :])
+            for half in range(2)
+        ]
+
+    fields = children(side_by_side(current), 6)
+    fields = [tile for j in range(2) for tile in children(fields[j], 4 + j)]
+    fields = [tile for j in range(4) for tile in children(fields[j], j)]
+    for quad in range(8):
+        high, low = halves(jnp.concatenate([jnp.where(group == k, fields[quad], 0.0) for k in range(4)], axis=0))
+        basis = v_ref[4 * quad : 4 * quad + 4].reshape(128, 256)
+        done = dot(jnp.concatenate([high, low], axis=1), jnp.concatenate([basis, basis], axis=0))
         for k in range(4):
-            lanes = pl.ds((4 * group + k) * 256, 256)
-            out_ref[:, lanes] = out_ref[:, lanes] + both[16 * k : 16 * k + 16]
+            lanes = pl.ds((4 * quad + k) * 256, 256)
+            out_ref[:, lanes] = near_ref[4 * quad + k] + done[16 * k : 16 * k + 16]
 
     wait_all(lifts_ref.at[pl.ds(0, 7)], in_send)
     wait_all(upper_ref.at[pl.ds(0, 15)], out_send)
@@ -520,8 +551,10 @@
             pltpu.VMEM((16, 16, 1024), F32),
             pltpu.VMEM((1008, 256), F32),
             pltpu.VMEM((1008, 128), F32),
-            pltpu.VMEM((512, 1024), BF16),
-            pltpu.VMEM((512, 1024), BF16),
+            pltpu.VMEM((256, 1024), BF16),
+            pltpu.VMEM((256, 1024), BF16),
+            pltpu.VMEM((32, 16, 256), F32),
+            pltpu.VMEM((7, 256, 128), BF16),
             pltpu.SemaphoreType.DMA((3, 8)),
             pltpu.SemaphoreType.DMA((5,)),
             pltpu.SemaphoreType.DMA,

time: 35.8 us -> 34.4 us (0.961)
  Pallas kernels: 33.8 us -> 32.4 us
    pallas_call x1, Pallas kernels: 33.8 us -> 32.4 us  [local(): pl.pallas_call(kernel, out_shape=jax.ShapeDtypeStruct((16, 8192), F32), i...]
where the time goes in v4:
time: 34.4 us; the launch traced here: 34.3 us
  Pallas kernels  32.4 us (94%)
  local copies, waits for them, and re-layouts  1.87 us (5%)
    pallas_call x1, Pallas kernels, local(): pl.pallas_call(kernel, out_shape=jax.ShapeDtypeStruct((16, 8192), F32), i...  32.4 us
    unnamed x1, local copies, waits for them, and re-layouts  1.87 us

profile of v4, /device:TPU:1, one launch (start us, length us, event | category | flops | bytes accessed | tf_op | source)
XLA Modules:
  0.0 34.3 jit_solution(3729380177350089799)
XLA Ops:
  0.0 32.4 %whole.1 = f32[16,8192]{1,0:T(8,128)} custom-call(bf16[16,8192]{1,0:T(8,128)(2,1)} %x_ref.1, bf16[32,32,256]{2,1,0:T(8,128)(2,1)} %v_ref.1, bf16[63,1024]{1,0:T(8,128)(2,1)} %e_ref.1, bf16[120,1024]{1,0:T(8,128)(2,1)} %ut_ref.1, s32[8,63]{1,0:T(8,128)} %bitcast.5, s32[8,63]{1,0:T(8,128)} %bitcast.6, s32[8,768]{1,0:T(8,128)} %constant.2.clone.lane_ref, ...), custom_call_target="tpu_custom_call" | custom-call | tf_op jit(solution)/shard_map/whole/pallas_call | solution.py:522
  32.4 1.9 %copy.16 = f32[16,8192]{1,0:T(8,128)} copy(f32[16,8192]{1,0:T(8,128)} %whole.1) | data formatting | bytes 1048576

commit v5 on v4

--- a/solution.py
+++ b/solution.py
@@ -310,23 +310,21 @@
     out = chosen(1040, 640, 128, *halves(part))
     for k in range(65):
         put(k - 32, 0, out[k * 16 : k * 16 + 16, :])
-    far_start(4)
     part = jnp.concatenate([prod_ref[448:480, j * 128 : j * 128 + 128] for j in range(4)], axis=0)
     out = chosen(528, 512, 128, *halves(part))
     for k in range(33):
         put(k - 16, 1, out[k * 16 : k * 16 + 16, :])
-    far_start(3)
     part = jnp.concatenate([prod_ref[384:448, j * 256 : j * 256 + 256] for j in range(2)], axis=0)
     out = chosen(272, 384, 128, *halves(part))
     for k in range(17):
         for j in range(2):
             put(k - 8, 2 + j, out[k * 16 : k * 16 + 16, j * 128 : j * 128 + 128])
-    far_start(2)
     out = chosen(144, 256, 128, *halves(prod_ref[256:384, :]))
     for k in range(9):
         for j in range(4):
             put(k - 4, 4 + j, out[k * 16 : k * 16 + 16, j * 128 : j * 128 + 128])
-    far_start(1)
+    for number in (1, 2, 3, 4):
+        far_start(number)
 
     couple(0, 32)
     out = chosen(160, 0, 256, *halves(prod_ref[0:256, :]))
@@ -337,6 +335,20 @@
                 put(k - 2, 8 + 4 * half + j, out[row : row + 16, j * 128 : j * 128 + 128])
     far_start(0)
 
+    index_copy.wait()
+    for k in range(2):
+        shock_copy(k).wait_recv()
+    for c in range(8):
+        for kind in range(2):
+            load(c, kind).wait()
+
+        @pl.loop(4 * c, 4 * c + 4, unroll=2)
+        def _(g):
+            total = dot(shock_ref[32 + g], self_v[g])
+            for j in range(3):
+                total = total + dot(shock_ref[index_s[j, g]], near_v[g, j])
+            near_ref[g] = total
+
     spot = iota((32, 1024), 1) // 32 == iota((32, 1024), 0)
     unit = jnp.where(iota((1024, 128), 0) % 32 == iota((1024, 128), 1) % 32, 1.0, 0.0).astype(BF16)
     parent_mask = iota((256, 128), 1) // 32 == iota((256, 128), 0) // 64
@@ -345,20 +357,6 @@
             row = ef_ref[pl.ds(8 * octet + k, 1), :]
             high_ref[pl.ds(32 * k, 32), :] = jnp.where(spot, row, 0.0).astype(BF16)
         stack_ref[octet] = jnp.where(parent_mask, dot(high_ref[pl.ds(0, 256), :], unit), 0.0).astype(BF16)
-
-    index_copy.wait()
-    for k in range(2):
-        shock_copy(k).wait_recv()
-    for c in range(8):
-        for kind in range(2):
-            load(c, kind).wait()
-
-        @pl.loop(4 * c, 4 * c + 4, unroll=2)
-        def _(g):
-            total = dot(shock_ref[32 + g], self_v[g])
-            for j in range(3):
-                total = total + dot(shock_ref[index_s[j, g]], near_v[g, j])
-            near_ref[g] = total
 
     wait_all(upper_ref.at[pl.ds(0, 15)], out_recv)
     mask = iota((256, 128), 1) // 32 == 2

time: 34.4 us -> 34.3 us (level)
  no operation moved by 1% of the time
where the time goes in v5:
time: 34.3 us; the launch traced here: 34.1 us
  Pallas kernels  32.2 us (94%)
  local copies, waits for them, and re-layouts  1.87 us (5%)
    pallas_call x1, Pallas kernels, local(): pl.pallas_call(kernel, out_shape=jax.ShapeDtypeStruct((16, 8192), F32), i...  32.2 us
    unnamed x1, local copies, waits for them, and re-layouts  1.87 us

profile of v5, /device:TPU:1, one launch (start us, length us, event | category | flops | bytes accessed | tf_op | source)
XLA Modules:
  0.0 34.1 jit_solution(2581581520315996403)
XLA Ops:
  0.0 32.2 %whole.1 = f32[16,8192]{1,0:T(8,128)} custom-call(bf16[16,8192]{1,0:T(8,128)(2,1)} %x_ref.1, bf16[32,32,256]{2,1,0:T(8,128)(2,1)} %v_ref.1, bf16[63,1024]{1,0:T(8,128)(2,1)} %e_ref.1, bf16[120,1024]{1,0:T(8,128)(2,1)} %ut_ref.1, s32[8,63]{1,0:T(8,128)} %bitcast.5, s32[8,63]{1,0:T(8,128)} %bitcast.6, s32[8,768]{1,0:T(8,128)} %constant.2.clone.lane_ref, ...), custom_call_target="tpu_custom_call" | custom-call | tf_op jit(solution)/shard_map/whole/pallas_call | solution.py:520
  32.2 1.9 %copy.16 = f32[16,8192]{1,0:T(8,128)} copy(f32[16,8192]{1,0:T(8,128)} %whole.1) | data formatting | bytes 1048576
